TPU v7x, 256 devices: a whole 4x4x8 slice. The times are simulated.
256 devices in a mesh: gx: 16 (over x_hi, y, core), gy: 8 (over z), comp: 2 (over x_lo).
Axes of the slice: x: 4 (x_hi: 2, x_lo: 2; x = x_hi * 2 + x_lo), y: 4, z: 8, core: 2. Of those that a mesh axis runs over, the one named last changes fastest.
Arguments:
- tracer: float32 [16, 640, 4096], P(None, 'gy', ('gx', 'comp')), may hold values from -6 to 6
- ocean_u: float32 [16, 640, 4096], P(None, 'gy', ('gx', 'comp')), may hold values from -6 to 6
- ocean_v: float32 [16, 640, 4096], P(None, 'gy', ('gx', 'comp')), may hold values from -6 to 6
- ocean_mask: int32 [640, 4096], P('gy', ('gx', 'comp')), may hold values 0 or 1
- diffusivity: float32 [16], replicated, may hold values from 0.02 to 0.2
- viscosity: float32 [16], replicated, may hold values from 0.02 to 0.2
- remap: float32 [16, 16], replicated, may hold values from -1.5 to 1.5
- fold_partner: int32 [4096], P(('gx', 'comp')), may hold values from 0 to 4095, as said below
- ice_u: float32 [640, 4096], P(('gy', 'comp'), 'gx'), may hold values from -3 to 3
- ice_v: float32 [640, 4096], P(('gy', 'comp'), 'gx'), may hold values from -3 to 3
- ice_mass: float32 [640, 4096], P(('gy', 'comp'), 'gx'), may hold values from 0.5 to 4
- ice_strength: float32 [640, 4096], P(('gy', 'comp'), 'gx'), may hold values from 0.2 to 2
- ice_mask: int32 [640, 4096], P(('gy', 'comp'), 'gx'), may hold values 0 or 1
Outputs:
- new_tracer: float32 [16, 640, 4096], P(None, 'gy', ('gx', 'comp'))
- new_ocean_u: float32 [16, 640, 4096], P(None, 'gy', ('gx', 'comp'))
- new_ocean_v: float32 [16, 640, 4096], P(None, 'gy', ('gx', 'comp'))
- new_ice_u: float32 [640, 4096], P(('gy', 'comp'), 'gx')
- new_ice_v: float32 [640, 4096], P(('gy', 'comp'), 'gx')
Inputs may be any that keep to these rules, and one draw needn't show every extreme that they name: `fold_partner`: columns of zonal block k (blocks of 128 columns in order) pair with columns of block 31 - k; the partner of a column's partner is the column itself.
All inputs are finite; a program needn't handle non-finite values. No bound on the sum of `ocean_mask` or of `ice_mask` on one device may be relied on, other than what follows from the above.
Results may differ from a plain program's by a relative error of at most 0.000088.
Values sent between devices are 32-bit elements; how exact they have to be, the bound alone decides.
A program may use at most 64 MiB of HBM per device.

v0:
```python
import jax
import jax.numpy as jnp
from jax import lax
from jax.experimental import pallas as pl
from jax.experimental.pallas import tpu as pltpu
from jax.sharding import PartitionSpec as P

ITERS = 4
RELAX = 0.5
STEP_SIZE = 0.3
COUPLE = 0.5
MESH = pl.DeviceIdType.MESH

LEV = 16
ROWS = 80
HALF = 40
COLS = 128
NF = 10
NS = NF + 1
REACH = 2
SIDE = 2 * REACH + 1
BLOCKS = 2 * SIDE
TOP = 16
SPAN = 96
OWN_REACH = {2: 0, 3: 1}
MIRROR_REACH = {1: 0, 2: 1, 3: 2}
OWN_ROWS = (8, 2, 1)
MIRROR_ROWS = (4, 3, 2)
PLANES = 3 * LEV + 1


def kernel(
    blocks,
    gys,
    tracer,
    ocean_u,
    ocean_v,
    ocean_mask,
    diffusivity_in,
    viscosity_in,
    remap_in,
    fold_in,
    ice_u,
    ice_v,
    ice_mass,
    ice_strength,
    ice_mask,
    new_tracer,
    new_ocean_u,
    new_ocean_v,
    new_ice_u,
    new_ice_v,
    F,
    DH,
    DL,
    KK,
    O,
    X,
    AB,
    S,
    SAB,
    SS,
    S2,
    SS2,
    PE,
    PW,
    EB,
    WB,
    CP,
    RE,
    RW,
    GE,
    MK,
    OM,
    IM,
    IDX,
    diffusivity,
    viscosity,
    remap,
    remap_wide,
    fold_partner,
    in_sem,
    ice_sem,
    ice_send,
    ice_recv,
    edge_send,
    edge_recv,
    rim_send,
    rim_recv,
    strip_send,
    strip_recv,
    again_send,
    again_recv,
    out_sem,
    vel_send,
    vel_recv,
):
    gx, gy, comp = lax.axis_index("gx"), lax.axis_index("gy"), lax.axis_index("comp")
    me = gx * 2 + comp
    has_north = gy < gys - 1
    has_south = gy > 0
    is_top = gy == gys - 1

    def at(block, row):
        return {"gx": block // 2, "gy": row, "comp": lax.rem(block, 2)}

    def wrap(block):
        return lax.rem(block + 2 * blocks, blocks)

    east, west, mirror = wrap(me + 1), wrap(me - 1), blocks - 1 - me
    partner = at(gx * 2 + 1 - comp, gy)

    strips = [(SIDE + REACH, mirror, False, MIRROR_ROWS[0])]
    for d in (1, -1, 2, -2):
        strips.append((SIDE + REACH + d, wrap(mirror + d), d % 2 == 1, MIRROR_ROWS[abs(d)]))
        strips.append((REACH + d, wrap(me - d), False, OWN_ROWS[abs(d)]))

    barrier = pltpu.get_barrier_semaphore()

    def greet(target):
        pl.semaphore_signal(barrier, inc=1, device_id=target, device_id_type=MESH)

    greet(at(east, gy))
    greet(at(west, gy))

    @pl.when(has_north)
    def _():
        for block in (me, east, west):
            greet(at(block, gy + 1))

    @pl.when(has_south)
    def _():
        for block in (me, east, west):
            greet(at(block, gy - 1))

    @pl.when(is_top)
    def _():
        for _, block, own, _ in strips:
            if own:

                @pl.when(block != me)
                def _(block=block):
                    greet(at(block, gy))
            else:
                greet(at(block, gy))

    def load(src, dst, sem):
        copy = pltpu.make_async_copy(src, dst, sem)
        copy.start()
        return copy

    load_u = load(ocean_u, F.at[LEV : 2 * LEV, 8 : 8 + ROWS, :], in_sem.at[0])
    load_v = load(ocean_v, F.at[2 * LEV : 3 * LEV, 8 : 8 + ROWS, :], in_sem.at[1])
    load_t = load(tracer, F.at[0:LEV, 8 : 8 + ROWS, :], in_sem.at[3])
    small = [
        load(ocean_mask, OM, in_sem.at[2]),
        load(remap_in, remap, in_sem.at[4]),
        load(diffusivity_in, diffusivity, in_sem.at[5]),
        load(viscosity_in, viscosity, in_sem.at[6]),
        load(fold_in, fold_partner, in_sem.at[7]),
        load(remap_in, remap_wide, in_sem.at[8]),
    ]
    ice_in = (ice_u, ice_v, ice_mass, ice_strength, ice_mask)

    def ice_place(i, half):
        rows = pl.ds(pl.multiple_of(TOP + HALF * half, 8), HALF)
        if i == 4:
            return IM.at[pl.ds(pl.multiple_of(HALF * half, 8), HALF), :]
        return X.at[i, rows, 0:COLS]

    mine = pl.ds(pl.multiple_of(COLS * comp, COLS), COLS)
    other = pl.ds(pl.multiple_of(COLS * (1 - comp), COLS), COLS)
    ice_local = [load(ice_in[i].at[:, mine], ice_place(i, comp), ice_sem.at[i]) for i in range(5)]

    first8, last8 = slice(TOP, TOP + 8), slice(TOP + ROWS - 8, TOP + ROWS)
    south8, north8 = slice(TOP - 8, TOP), slice(TOP + ROWS, TOP + ROWS + 8)

    @pl.when(jnp.logical_not(has_south))
    def _():
        X[:, south8, 0:COLS] = jnp.zeros((NF, 8, COLS), jnp.float32)
        EB[0:8, :] = jnp.zeros((8, COLS), jnp.float32)
        WB[0:8, :] = jnp.zeros((8, COLS), jnp.float32)
        F[:, 0:8, :] = jnp.zeros((PLANES, 8, COLS), jnp.float32)

    @pl.when(is_top)
    def _():
        X[:, north8, 0:COLS] = jnp.zeros((NF, 8, COLS), jnp.float32)
        EB[88:96, :] = jnp.zeros((8, COLS), jnp.float32)
        WB[88:96, :] = jnp.zeros((8, COLS), jnp.float32)

    outer = jnp.zeros((NF, 8, 2 * COLS), jnp.float32)
    X[:, 0:8, :] = outer
    X[:, 104:112, :] = outer
    AB[:, 0:8, :] = outer[0:2]
    AB[:, 104:112, :] = outer[0:2]

    count = 2 + 3 * has_north.astype(jnp.int32) + 3 * has_south.astype(jnp.int32)
    strip_count = 0
    for _, block, own, _ in strips:
        strip_count = strip_count + ((block != me).astype(jnp.int32) if own else 1)
    count = count + is_top.astype(jnp.int32) * strip_count
    pl.semaphore_wait(barrier, count)

    def send(src, dst, send_sem, recv_sem, target):
        copy = pltpu.make_async_remote_copy(
            src_ref=src,
            dst_ref=dst,
            send_sem=send_sem,
            recv_sem=recv_sem,
            device_id=target,
            device_id_type=MESH,
        )
        return copy

    ice_away = []
    for i in range(5):
        copy = send(
            ice_in[i].at[:, other], ice_place(i, comp), ice_send.at[i], ice_recv.at[i], partner
        )
        copy.start()
        ice_away.append(copy)

    lane = lax.broadcasted_iota(jnp.int32, (1, COLS), 1)
    row8 = lax.broadcasted_iota(jnp.int32, (8, 1), 0)
    tile_rows = slice(TOP, TOP + ROWS)

    for copy in small:
        copy.wait()
    sea = OM[...].astype(jnp.float32)
    X[9, tile_rows, 0:COLS] = sea
    F[3 * LEV, 8 : 8 + ROWS, :] = sea
    for i, copy in ((0, load_u), (1, load_v)):
        copy.wait()
        base = jnp.zeros((ROWS, COLS), jnp.float32)
        spread = jnp.zeros((ROWS, COLS), jnp.float32)
        for l in range(LEV):
            weighted = remap[0, l] * F[LEV * (i + 1) + l, 8 : 8 + ROWS, :]
            base = base + weighted
            spread = spread + viscosity[l] * weighted
        X[5 + i, tile_rows, 0:COLS] = base
        X[7 + i, tile_rows, 0:COLS] = spread

    load_t.wait()
    row_n = send(F.at[:, 87:88, :], F.at[:, 7:8, :], edge_send.at[2], edge_recv.at[2], at(me, gy + 1))
    row_s = send(F.at[:, 8:9, :], F.at[:, 88:89, :], edge_send.at[3], edge_recv.at[3], at(me, gy - 1))
    row_f = send(F.at[:, 87:88, :], F.at[:, 88:89, :], edge_send.at[4], edge_recv.at[4], at(mirror, gy))

    @pl.when(has_north)
    def _():
        row_n.start()

    @pl.when(has_south)
    def _():
        row_s.start()

    @pl.when(is_top)
    def _():
        row_f.start()

    def pack(f, packed):
        return jnp.where((lane >> 1) == f, pltpu.roll(F[f, 8 : 8 + ROWS, :], 2 * f + 1, 1), packed)

    CP[...] = lax.fori_loop(0, PLANES, pack, jnp.zeros((ROWS, COLS), jnp.float32), unroll=7)
    col_to_e = send(CP, RW, edge_send.at[0], edge_recv.at[0], at(east, gy))
    col_to_w = send(CP, RE, edge_send.at[1], edge_recv.at[1], at(west, gy))
    col_to_e.start()
    col_to_w.start()

    lane2 = lax.broadcasted_iota(jnp.int32, (LEV, LEV * LEV), 1)
    weights = jnp.zeros((LEV, LEV * LEV), jnp.float32)
    for l in range(LEV):
        weights = jnp.where((lane2 >> 4) == l, remap_wide[:, l : l + 1], weights)
    high = weights.astype(jnp.bfloat16).astype(jnp.float32)
    low = weights - high
    diagonal = (lane2 & 15) == lax.broadcasted_iota(jnp.int32, (LEV, LEV * LEV), 0)
    for k in range(LEV):
        rows = slice(LEV * k, LEV * (k + 1))
        high_k = jnp.where(diagonal, high[k : k + 1], 0.0).astype(jnp.bfloat16)
        KK[rows, 0:256] = high_k
        KK[rows, 256:512] = jnp.where(diagonal, low[k : k + 1], 0.0).astype(jnp.bfloat16)
        KK[rows, 512:768] = high_k

    for i in range(5):
        ice_local[i].wait()
        ice_away[i].wait_recv()
    X[4, tile_rows, 0:COLS] = IM[...].astype(jnp.float32)

    pack_e = jnp.zeros((ROWS, COLS), jnp.float32)
    pack_w = jnp.zeros((ROWS, COLS), jnp.float32)
    for f in range(NF):
        value = X[f, tile_rows, 0:COLS]
        keep = (lane >= 8 * f) & (lane < 8 * f + 8)
        pack_e = jnp.where(keep, pltpu.roll(value, 8 * f + 8, 1), pack_e)
        pack_w = jnp.where(keep, pltpu.roll(value, 8 * f, 1) if f else value, pack_w)
    PE[...] = pack_e
    PW[...] = pack_w
    to_e = send(PE, WB.at[8 : 8 + ROWS], rim_send.at[0], rim_recv.at[0], at(east, gy))
    to_w = send(PW, EB.at[8 : 8 + ROWS], rim_send.at[1], rim_recv.at[1], at(west, gy))
    to_n = [
        send(X.at[:, last8, 0:COLS], X.at[:, south8, 0:COLS], rim_send.at[2], rim_recv.at[2], at(me, gy + 1)),
        send(PE.at[ROWS - 8 : ROWS], WB.at[0:8], rim_send.at[3], rim_recv.at[3], at(east, gy + 1)),
        send(PW.at[ROWS - 8 : ROWS], EB.at[0:8], rim_send.at[4], rim_recv.at[4], at(west, gy + 1)),
    ]
    to_s = [
        send(X.at[:, first8, 0:COLS], X.at[:, north8, 0:COLS], rim_send.at[5], rim_recv.at[5], at(me, gy - 1)),
        send(PE.at[0:8], WB.at[88:96], rim_send.at[6], rim_recv.at[6], at(east, gy - 1)),
        send(PW.at[0:8], EB.at[88:96], rim_send.at[7], rim_recv.at[7], at(west, gy - 1)),
    ]

    def strip_ends(src, dst, slot, rows):
        kept = slice(8 - rows, 8)
        return src.at[:, kept, :], dst.at[:, kept, COLS * slot : COLS * (slot + 1)]

    def strip_copy(again, slot, block, rows):
        src, dst = strip_ends(SS2, S2, slot, rows) if again else strip_ends(SS, S, slot, rows)
        sent, received = (again_send, again_recv) if again else (strip_send, strip_recv)
        return send(src, dst, sent.at[slot], received.at[slot], at(block, gy))

    def strips_start(again):
        for slot, block, own, rows in strips:
            if own:

                @pl.when(block != me)
                def _(slot=slot, block=block, rows=rows):
                    strip_copy(again, slot, block, rows).start()

                @pl.when(block == me)
                def _(slot=slot, rows=rows):
                    src, dst = strip_ends(SS2, S2, slot, rows) if again else strip_ends(SS, S, slot, rows)
                    pltpu.make_async_copy(src, dst, (again_recv if again else strip_recv).at[slot]).start()
            else:
                strip_copy(again, slot, block, rows).start()

    def strips_arrive(again):
        for slot, block, own, rows in strips:
            strip_copy(again, slot, block, rows).wait_recv()

    def strips_sent(again):
        for slot, block, own, rows in strips:
            if own:

                @pl.when(block != me)
                def _(slot=slot, block=block, rows=rows):
                    strip_copy(again, slot, block, rows).wait_send()
            else:
                strip_copy(again, slot, block, rows).wait_send()

    middle = slice(COLS * REACH, COLS * (REACH + 1))

    @pl.when(is_top)
    def _():
        SS[0:NF] = X[0:NF, last8, 0:COLS]
        inside = fold_partner[...] - COLS * mirror
        SS[NF] = jnp.broadcast_to(inside.astype(jnp.float32), (8, COLS))
        strips_start(False)

    to_e.start()
    to_w.start()

    @pl.when(has_north)
    def _():
        for copy in to_n:
            copy.start()

    @pl.when(has_south)
    def _():
        for copy in to_s:
            copy.start()

    col_to_e.wait()
    col_to_w.wait()

    @pl.when(has_north)
    def _():
        row_n.wait_send()
        row_s.wait_recv()

    @pl.when(has_south)
    def _():
        row_s.wait_send()
        row_n.wait_recv()


    @pl.when(is_top)
    def _():
        row_f.wait()
        inside = jnp.broadcast_to(fold_partner[...] - COLS * mirror, (8, COLS))

        def fold_edge(f, carry):
            taken = jnp.take_along_axis(F[f, 88:96, :], inside, axis=1, mode="promise_in_bounds")
            F[f, 88:96, :] = jnp.where((f < LEV) | (f == 3 * LEV), taken, -taken)
            return carry

        lax.fori_loop(0, PLANES, fold_edge, 0, unroll=7)

    GE[...] = jnp.where((lane & 1) == 0, pltpu.roll(RE[...], COLS - 1, 1), pltpu.roll(RW[...], 1, 1))

    def plane_sides(f):
        value = F[f, 8 : 8 + ROWS, :]
        edges = pltpu.roll(GE[...], COLS - 1 - 2 * f, 1)
        to_east = jnp.where(lane == COLS - 1, edges, pltpu.roll(value, COLS - 1, 1))
        to_west = jnp.where(lane == 0, edges, pltpu.roll(value, 1, 1))
        return value, to_east, to_west, F[f, 9 : 9 + ROWS, :], F[f, 7 : 7 + ROWS, :]

    seas = plane_sides(3 * LEV)
    degree = jnp.zeros((ROWS, COLS), jnp.float32)
    for i in range(4):
        weight = seas[0] * seas[i + 1]
        MK[i] = weight
        degree = degree + weight
    MK[4] = degree

    def diffuse(g):
        coefficient = diffusivity if g == 0 else viscosity

        def one(l, carry):
            f = g * LEV + l
            value, to_east, to_west, to_north, to_south = plane_sides(f)
            total = MK[0] * to_east + MK[1] * to_west + MK[2] * to_north + MK[3] * to_south
            new = value + coefficient[l] * (total - MK[4] * value)
            high = new.astype(jnp.bfloat16)
            DH[f] = high
            DL[f] = (new - high.astype(jnp.float32)).astype(jnp.bfloat16)
            return carry

        lax.fori_loop(0, LEV, one, 0, unroll=4)

    def regrid(g):
        planes = slice(g * LEV, (g + 1) * LEV)
        pieces = range(0, ROWS, LEV)
        high = jnp.concatenate([DH[planes, r : r + LEV, :].reshape(LEV * LEV, COLS) for r in pieces], axis=1)
        low = jnp.concatenate([DL[planes, r : r + LEV, :].reshape(LEV * LEV, COLS) for r in pieces], axis=1)
        new = jnp.dot(KK[...], jnp.concatenate([high, high, low], axis=0), preferred_element_type=jnp.float32)
        for i, r in enumerate(pieces):
            O[planes, r : r + LEV, :] = new[:, COLS * i : COLS * (i + 1)].reshape(LEV, LEV, COLS)

    outs = (new_tracer, new_ocean_u, new_ocean_v)

    def store(g):
        copy = pltpu.make_async_copy(O.at[g * LEV : (g + 1) * LEV], outs[g], out_sem.at[g])
        copy.start()
        return copy

    diffuse(0)
    diffuse(1)
    diffuse(2)

    to_e.wait()
    to_w.wait()

    @pl.when(has_north)
    def _():
        for copy in to_n:
            copy.wait_send()
        for copy in to_s:
            copy.wait_recv()

    @pl.when(has_south)
    def _():
        for copy in to_s:
            copy.wait_send()
        for copy in to_n:
            copy.wait_recv()

    for f in range(NF):
        from_e = pltpu.roll(EB[...], COLS - 8 * f, 1) if f else EB[...]
        from_w = pltpu.roll(WB[...], COLS - 8 - 8 * f, 1)
        X[f, 8 : 8 + SPAN, COLS : 2 * COLS] = jnp.where(
            lane < 8, from_e, jnp.where(lane >= COLS - 8, from_w, 0.0)
        )

    def inside_of(i):
        return IDX[:, COLS * i : COLS * (i + 1)]

    def fold_block(ref, f, i, sign):
        j = BLOCKS - 1 - i
        value = ref[f, :, COLS * j : COLS * (j + 1)]
        taken = jnp.take_along_axis(value, inside_of(i), axis=1, mode="promise_in_bounds")
        return taken if sign > 0 else -taken

    def close_top(ref, f, strip_ref, sf, sign):
        own = fold_block(strip_ref, sf, REACH, sign)
        to_the_e = fold_block(strip_ref, sf, REACH + 1, sign)
        to_the_w = fold_block(strip_ref, sf, REACH - 1, sign)
        ref[f, 96:97, 0:COLS] = own[7:8]
        ref[f, 96:97, COLS : 2 * COLS] = jnp.where(lane < COLS // 2, to_the_e, to_the_w)[7:8]

    @pl.when(is_top)
    def _():
        S[:, :, middle] = SS[...]
        strips_arrive(False)
        IDX[...] = jnp.broadcast_to(S[NF, 7:8, :], IDX.shape).astype(jnp.int32)
        for f, sign in ((7, -1), (8, -1), (9, 1)):
            close_top(X, f, S, f, sign)

    def window(first, reach):
        middle = first + REACH
        low, high = middle - reach, middle + reach + 1
        wide_low, wide_high = max(low - 1, first), min(high + 1, first + SIDE)
        return low, high, wide_low, wide_high

    def strip_sides(ref, f, win, sign):
        low, high, wide_low, wide_high = win
        wide = ref[f, :, COLS * wide_low : COLS * wide_high]
        length = COLS * (wide_high - wide_low)
        cut = slice(COLS * (low - wide_low), COLS * (high - wide_low))
        value = wide[:, cut]
        to_east = pltpu.roll(wide, length - 1, 1)[:, cut]
        to_west = pltpu.roll(wide, 1, 1)[:, cut]
        folded = jnp.concatenate([fold_block(ref, f, i, sign) for i in range(low, high)], axis=1)
        to_north = jnp.where(row8 == 7, folded, pltpu.roll(value, 7, 0))
        to_south = pltpu.roll(value, 1, 0)
        return value, to_east, to_west, to_north, to_south

    def windows(left):
        found = []
        if left in OWN_REACH:
            found.append(window(0, OWN_REACH[left]))
        if left in MIRROR_REACH:
            found.append(window(SIDE, MIRROR_REACH[left]))
        return found

    def lap_of(seas, values):
        total = seas[1] * (values[1] - values[0])
        for i in range(2, 5):
            total = total + seas[i] * (values[i] - values[0])
        return total * seas[0]

    SHARE = STEP_SIZE / (1.0 + STEP_SIZE)
    KEEP = 1.0 / (1.0 + STEP_SIZE)

    def ready(ref, rows, cols, surfaces):
        present = ref[4, rows, cols]
        ref[5, rows, cols] = SHARE * present * surfaces[0]
        ref[6, rows, cols] = SHARE * present * surfaces[1]
        mass = ref[2, rows, cols]
        ref[2, rows, cols] = 0.5 * SHARE * present / jnp.where(mass > 0.0, mass, 1.0)
        ref[4, rows, cols] = KEEP * present

    def strips_ready():
        for win in windows(2):
            cols = slice(COLS * win[0], COLS * win[1])
            seas = strip_sides(S, 9, win, 1)
            surfaces = [
                S[5 + i, :, cols] + lap_of(seas, strip_sides(S, 7 + i, win, -1)) for i in range(2)
            ]
            ready(S, slice(0, 8), cols, surfaces)
        S[3] = S[3] * (RELAX / (1.0 + RELAX))

    def main_sides(ref, f, start, size):
        value = ref[f, start : start + size, :]
        return (
            value,
            pltpu.roll(value, 2 * COLS - 1, 1),
            pltpu.roll(value, 1, 1),
            ref[f, start + 1 : start + size + 1, :],
            ref[f, start - 1 : start + size - 1, :],
        )

    CHUNK = 24
    chunks = range(8, 8 + SPAN, CHUNK)

    def tile_ready():
        for start in chunks:
            rows = slice(start, start + CHUNK)
            seas = main_sides(X, 9, start, CHUNK)
            surfaces = [X[5 + i, rows, :] + lap_of(seas, main_sides(X, 7 + i, start, CHUNK)) for i in range(2)]
            ready(X, rows, slice(0, 2 * COLS), surfaces)
            X[3, rows, :] = X[3, rows, :] * (RELAX / (1.0 + RELAX))

    def stress(u, v, third, old):
        twice_d = (u[1] - u[2]) + (v[3] - v[4])
        twice_h = (u[3] - u[4]) + (v[1] - v[2])
        viscous = third * lax.rsqrt(twice_d * twice_d + 0.25 * (twice_h * twice_h) + 0.04)
        a = viscous * twice_d - third
        b = viscous * twice_h
        if old is not None:
            a = a + old[0] * (1.0 / (1.0 + RELAX))
            b = b + old[1] * (1.0 / (1.0 + RELAX))
        return a, b

    def push(ref, vel, rows, cols, a, b):
        keep, mobility = ref[4, rows, cols], ref[2, rows, cols]
        new_u = keep * vel[0, rows, cols] + mobility * ((a[1] - a[2]) + (b[3] - b[4])) + ref[5, rows, cols]
        new_v = keep * vel[1, rows, cols] + mobility * ((b[1] - b[2]) + (a[3] - a[4])) + ref[6, rows, cols]
        vel[0, rows, cols] = new_u
        vel[1, rows, cols] = new_v

    every = slice(0, 8)

    def tile_stress(first):
        for start in chunks:
            rows = slice(start, start + CHUNK)
            u, v = main_sides(X, 0, start, CHUNK), main_sides(X, 1, start, CHUNK)
            old = None if first else (AB[0, rows, :], AB[1, rows, :])
            AB[0, rows, :], AB[1, rows, :] = stress(u, v, X[3, rows, :], old)

    def tile_push():
        for start in chunks:
            rows = slice(start, start + CHUNK)
            push(X, X, rows, slice(0, 2 * COLS), main_sides(AB, 0, start, CHUNK), main_sides(AB, 1, start, CHUNK))

    def tile_cycle(cycle, carry):
        tile_stress(False)
        tile_push()
        return carry

    def top_cycles(cycles):
        vel, sig, i_a, i_b = (S, SAB, 0, 1) if cycles[0] == 0 else (S2, S2, 2, 3)
        for cycle in cycles:
            left = 3 if cycle == cycles[0] else 1
            close_top(X, 0, vel, 0, -1)
            close_top(X, 1, vel, 1, -1)
            for win in windows(left):
                cols = slice(COLS * win[0], COLS * win[1])
                u, v = strip_sides(vel, 0, win, -1), strip_sides(vel, 1, win, -1)
                old = (sig[i_a, :, cols], sig[i_b, :, cols]) if cycle else None
                sig[i_a, :, cols], sig[i_b, :, cols] = stress(u, v, S[3, :, cols], old)
            tile_stress(cycle == 0)
            close_top(AB, 0, sig, i_a, 1)
            close_top(AB, 1, sig, i_b, 1)
            for win in windows(left - 1):
                cols = slice(COLS * win[0], COLS * win[1])
                push(S, vel, every, cols, strip_sides(sig, i_a, win, 1), strip_sides(sig, i_b, win, 1))
            tile_push()

    @pl.when(is_top)
    def _():
        strips_ready()
        tile_ready()
        top_cycles((0, 1))
        SS2[0:2] = X[0:2, last8, 0:COLS]
        SS2[2:4] = AB[:, last8, 0:COLS]
        S2[:, :, middle] = SS2[...]
        strips_start(True)

    @pl.when(jnp.logical_not(is_top))
    def _():
        tile_ready()
        AB[:, 8 : 8 + SPAN, :] = jnp.zeros((2, SPAN, 2 * COLS), jnp.float32)
        lax.fori_loop(0, 2, tile_cycle, 0)

    regrid(0)
    stores = [store(0)]
    regrid(1)

    @pl.when(is_top)
    def _():
        strips_arrive(True)
        to_the_e = S2[0:2, 7:8, COLS * (REACH + 1) : COLS * (REACH + 2)]
        to_the_w = S2[0:2, 7:8, COLS * (REACH - 1) : COLS * REACH]
        X[0:2, TOP + ROWS - 1 : TOP + ROWS, COLS : 2 * COLS] = jnp.where(lane < COLS // 2, to_the_e, to_the_w)
        top_cycles((2, 3))

    @pl.when(jnp.logical_not(is_top))
    def _():
        lax.fori_loop(0, 2, tile_cycle, 0)

    away = pl.ds(pl.multiple_of(TOP + HALF * (1 - comp), 8), HALF)
    here = pl.ds(pl.multiple_of(TOP + HALF * comp, 8), HALF)
    ice_out = (new_ice_u, new_ice_v)
    vel_away, vel_here = [], []
    for i in range(2):
        copy = send(X.at[i, away, 0:COLS], ice_out[i].at[:, mine], vel_send.at[i], vel_recv.at[i], partner)
        copy.start()
        vel_away.append(copy)
        copy = pltpu.make_async_copy(X.at[i, here, 0:COLS], ice_out[i].at[:, mine], out_sem.at[3 + i])
        copy.start()
        vel_here.append(copy)

    for i in range(2):
        g = i + 1
        if g == 2:
            regrid(g)
        tau = X[i, tile_rows, 0:COLS] - X[5 + i, tile_rows, 0:COLS] * (1.0 / SHARE)
        O[g * LEV] = O[g * LEV] + COUPLE * (X[9, tile_rows, 0:COLS] * tau)
        stores.append(store(g))

    @pl.when(is_top)
    def _():
        strips_sent(False)
        strips_sent(True)

    for copy in ice_away:
        copy.wait_send()
    for copy in vel_away:
        copy.wait()
    for copy in vel_here + stores:
        copy.wait()


def deliver(*refs):
    count = len(refs) // 2
    sems = refs[-1]
    copies = [pltpu.make_async_copy(refs[i], refs[count + i], sems.at[i]) for i in range(count)]
    for copy in copies:
        copy.start()
    for copy in copies:
        copy.wait()


def solution(mesh):
    blocks = mesh.shape["gx"] * 2
    gys = mesh.shape["gy"]
    ocean = P(None, "gy", ("gx", "comp"))
    flat = P("gy", ("gx", "comp"))
    ice = P(("gy", "comp"), "gx")
    in_specs = (ocean, ocean, ocean, flat, P(), P(), P(), P(("gx", "comp")), ice, ice, ice, ice, ice)
    out_specs = (ocean, ocean, ocean, ice, ice)

    def body(tracer, ocean_u, ocean_v, ocean_mask, diffusivity, viscosity, remap, fold_partner, *ice_fields):
        f32 = jnp.float32
        anywhere = pl.BlockSpec(memory_space=pl.ANY)
        main_memory = pl.BlockSpec(memory_space=pltpu.HBM)
        vmem = pltpu.VMEM
        dma = pltpu.SemaphoreType.DMA
        ocean_shape = jax.ShapeDtypeStruct(tracer.shape, f32)
        ice_shape = jax.ShapeDtypeStruct(ice_fields[0].shape, f32)

        def step(*args):
            kernel(blocks, gys, *args)

        shapes = (ocean_shape, ocean_shape, ocean_shape, ice_shape, ice_shape)
        results = pl.pallas_call(
            step,
            out_shape=shapes,
            in_specs=[main_memory] * 13,
            out_specs=(anywhere,) * 5,
            scratch_shapes=[
                vmem((PLANES, 96, COLS), f32),
                vmem((3 * LEV, ROWS, COLS), jnp.bfloat16),
                vmem((3 * LEV, ROWS, COLS), jnp.bfloat16),
                vmem((LEV * LEV, 3 * LEV * LEV), jnp.bfloat16),
                vmem((3 * LEV, ROWS, COLS), f32),
                vmem((NF, 112, 2 * COLS), f32),
                vmem((2, 112, 2 * COLS), f32),
                vmem((NS, 8, BLOCKS * COLS), f32),
                vmem((2, 8, BLOCKS * COLS), f32),
                vmem((NS, 8, COLS), f32),
                vmem((4, 8, BLOCKS * COLS), f32),
                vmem((4, 8, COLS), f32),
                vmem((ROWS, COLS), f32),
                vmem((ROWS, COLS), f32),
                vmem((SPAN, COLS), f32),
                vmem((SPAN, COLS), f32),
                vmem((ROWS, COLS), f32),
                vmem((ROWS, COLS), f32),
                vmem((ROWS, COLS), f32),
                vmem((ROWS, COLS), f32),
                vmem((5, ROWS, COLS), f32),
                vmem((ROWS, COLS), jnp.int32),
                vmem((ROWS, COLS), jnp.int32),
                vmem((8, BLOCKS * COLS), jnp.int32),
                pltpu.SMEM((LEV,), f32),
                pltpu.SMEM((LEV,), f32),
                pltpu.SMEM((LEV, LEV), f32),
                vmem((LEV, LEV), f32),
                vmem((1, COLS), jnp.int32),
                dma((9,)),
                dma((5,)),
                dma((5,)),
                dma((5,)),
                dma((5,)),
                dma((5,)),
                dma((8,)),
                dma((8,)),
                dma((BLOCKS,)),
                dma((BLOCKS,)),
                dma((BLOCKS,)),
                dma((BLOCKS,)),
                dma((5,)),
                dma((2,)),
                dma((2,)),
            ],
            compiler_params=pltpu.CompilerParams(
                collective_id=0, has_side_effects=True, vmem_limit_bytes=32 * 1024 * 1024
            ),
        )(
            *[
                pltpu.with_memory_space_constraint(value, pltpu.HBM)
                for value in (
                    tracer,
                    ocean_u,
                    ocean_v,
                    ocean_mask,
                    diffusivity,
                    viscosity,
                    remap,
                    fold_partner.reshape(1, COLS),
                    *ice_fields,
                )
            ]
        )
        return pl.pallas_call(
            deliver,
            out_shape=shapes,
            in_specs=[anywhere] * 5,
            out_specs=(main_memory,) * 5,
            scratch_shapes=[dma((5,))],
            compiler_params=pltpu.CompilerParams(vmem_limit_bytes=1024 * 1024),
        )(*results)

    return jax.shard_map(body, mesh=mesh, in_specs=in_specs, out_specs=out_specs, check_vma=False)
```

profile of v0, /device:TPU:224, one launch (start us, length us, event | category | flops | bytes accessed | tf_op | source)
XLA Modules:
  0.0 28.1 jit_solution(16054154263140272078)
XLA Ops:
  0.6 26.2 %shard_map.164 = (f32[16,80,128]{2,1,0:T(8,128)S(1)}, f32[16,80,128]{2,1,0:T(8,128)S(1)}, f32[16,80,128]{2,1,0:T(8,128)S(1)}, f32[40,256]{1,0:T(8,128)S(1)}, f32[40,256]{1,0:T(8,128)S(1)}) custom-call(f32[16,80,128]{2,1,0:T(8,128)} %args_0_.4, f32[16,80,128]{2,1,0:T(8,128)} %args_1_.4, f32[16,80,128]{2,1,0:T(8,128)} %args_2_.4, s32[80,128]{1,0:T(8,128)} %args_3_.4, ...), custom_call_target="tpu_custom_call" | custom-call | tf_op jit(solution)/shard_map/pallas_call | solution.py:724
  26.8 1.3 %shard_map.165 = (f32[16,80,128]{2,1,0:T(8,128)}, f32[16,80,128]{2,1,0:T(8,128)}, f32[16,80,128]{2,1,0:T(8,128)}, f32[40,256]{1,0:T(8,128)}, f32[40,256]{1,0:T(8,128)}) custom-call(f32[16,80,128]{2,1,0:T(8,128)S(1)} %get-tuple-element.10.refs_0_, f32[16,80,128]{2,1,0:T(8,128)S(1)} %get-tuple-element.11.refs_1_, ...), custom_call_target="tpu_custom_call" | custom-call | tf_op jit(solution)/shard_map/pallas_call | solution.py:794
where the time goes:
time: 28.2 us; the launch traced here: 28.1 us
  Pallas kernels  27.5 us (98%)
  between operations  0.64 us (2%)
    pallas_call x1, Pallas kernels, body(): pl.pallas_call(step, out_shape=shapes, in_specs=[main_memory] * 13, out_s...  26.2 us
    pallas_call x1, Pallas kernels, body(): pl.pallas_call(deliver, out_shape=shapes, in_specs=[anywhere] * 5, out_sp...  1.32 us

commit v1 on v0

--- a/solution.py
+++ b/solution.py
@@ -57,6 +57,8 @@
     O,
     X,
     AB,
+    XT,
+    ABT,
     S,
     SAB,
     SS,
@@ -191,8 +193,7 @@
     outer = jnp.zeros((NF, 8, 2 * COLS), jnp.float32)
     X[:, 0:8, :] = outer
     X[:, 104:112, :] = outer
-    AB[:, 0:8, :] = outer[0:2]
-    AB[:, 104:112, :] = outer[0:2]
+    AB[...] = jnp.zeros((2, 112, 2 * COLS), jnp.float32)
 
     count = 2 + 3 * has_north.astype(jnp.int32) + 3 * has_south.astype(jnp.int32)
     strip_count = 0
@@ -347,103 +348,26 @@
 
     middle = slice(COLS * REACH, COLS * (REACH + 1))
 
+    to_e.start()
+    to_w.start()
+
+    @pl.when(has_north)
+    def _():
+        for copy in to_n:
+            copy.start()
+
+    @pl.when(has_south)
+    def _():
+        for copy in to_s:
+            copy.start()
+
     @pl.when(is_top)
     def _():
         SS[0:NF] = X[0:NF, last8, 0:COLS]
         inside = fold_partner[...] - COLS * mirror
         SS[NF] = jnp.broadcast_to(inside.astype(jnp.float32), (8, COLS))
+        S[:, :, middle] = SS[...]
         strips_start(False)
-
-    to_e.start()
-    to_w.start()
-
-    @pl.when(has_north)
-    def _():
-        for copy in to_n:
-            copy.start()
-
-    @pl.when(has_south)
-    def _():
-        for copy in to_s:
-            copy.start()
-
-    col_to_e.wait()
-    col_to_w.wait()
-
-    @pl.when(has_north)
-    def _():
-        row_n.wait_send()
-        row_s.wait_recv()
-
-    @pl.when(has_south)
-    def _():
-        row_s.wait_send()
-        row_n.wait_recv()
-
-
-    @pl.when(is_top)
-    def _():
-        row_f.wait()
-        inside = jnp.broadcast_to(fold_partner[...] - COLS * mirror, (8, COLS))
-
-        def fold_edge(f, carry):
-            taken = jnp.take_along_axis(F[f, 88:96, :], inside, axis=1, mode="promise_in_bounds")
-            F[f, 88:96, :] = jnp.where((f < LEV) | (f == 3 * LEV), taken, -taken)
-            return carry
-
-        lax.fori_loop(0, PLANES, fold_edge, 0, unroll=7)
-
-    GE[...] = jnp.where((lane & 1) == 0, pltpu.roll(RE[...], COLS - 1, 1), pltpu.roll(RW[...], 1, 1))
-
-    def plane_sides(f):
-        value = F[f, 8 : 8 + ROWS, :]
-        edges = pltpu.roll(GE[...], COLS - 1 - 2 * f, 1)
-        to_east = jnp.where(lane == COLS - 1, edges, pltpu.roll(value, COLS - 1, 1))
-        to_west = jnp.where(lane == 0, edges, pltpu.roll(value, 1, 1))
-        return value, to_east, to_west, F[f, 9 : 9 + ROWS, :], F[f, 7 : 7 + ROWS, :]
-
-    seas = plane_sides(3 * LEV)
-    degree = jnp.zeros((ROWS, COLS), jnp.float32)
-    for i in range(4):
-        weight = seas[0] * seas[i + 1]
-        MK[i] = weight
-        degree = degree + weight
-    MK[4] = degree
-
-    def diffuse(g):
-        coefficient = diffusivity if g == 0 else viscosity
-
-        def one(l, carry):
-            f = g * LEV + l
-            value, to_east, to_west, to_north, to_south = plane_sides(f)
-            total = MK[0] * to_east + MK[1] * to_west + MK[2] * to_north + MK[3] * to_south
-            new = value + coefficient[l] * (total - MK[4] * value)
-            high = new.astype(jnp.bfloat16)
-            DH[f] = high
-            DL[f] = (new - high.astype(jnp.float32)).astype(jnp.bfloat16)
-            return carry
-
-        lax.fori_loop(0, LEV, one, 0, unroll=4)
-
-    def regrid(g):
-        planes = slice(g * LEV, (g + 1) * LEV)
-        pieces = range(0, ROWS, LEV)
-        high = jnp.concatenate([DH[planes, r : r + LEV, :].reshape(LEV * LEV, COLS) for r in pieces], axis=1)
-        low = jnp.concatenate([DL[planes, r : r + LEV, :].reshape(LEV * LEV, COLS) for r in pieces], axis=1)
-        new = jnp.dot(KK[...], jnp.concatenate([high, high, low], axis=0), preferred_element_type=jnp.float32)
-        for i, r in enumerate(pieces):
-            O[planes, r : r + LEV, :] = new[:, COLS * i : COLS * (i + 1)].reshape(LEV, LEV, COLS)
-
-    outs = (new_tracer, new_ocean_u, new_ocean_v)
-
-    def store(g):
-        copy = pltpu.make_async_copy(O.at[g * LEV : (g + 1) * LEV], outs[g], out_sem.at[g])
-        copy.start()
-        return copy
-
-    diffuse(0)
-    diffuse(1)
-    diffuse(2)
 
     to_e.wait()
     to_w.wait()
@@ -482,16 +406,8 @@
         own = fold_block(strip_ref, sf, REACH, sign)
         to_the_e = fold_block(strip_ref, sf, REACH + 1, sign)
         to_the_w = fold_block(strip_ref, sf, REACH - 1, sign)
-        ref[f, 96:97, 0:COLS] = own[7:8]
-        ref[f, 96:97, COLS : 2 * COLS] = jnp.where(lane < COLS // 2, to_the_e, to_the_w)[7:8]
-
-    @pl.when(is_top)
-    def _():
-        S[:, :, middle] = SS[...]
-        strips_arrive(False)
-        IDX[...] = jnp.broadcast_to(S[NF, 7:8, :], IDX.shape).astype(jnp.int32)
-        for f, sign in ((7, -1), (8, -1), (9, 1)):
-            close_top(X, f, S, f, sign)
+        ref[f, 24:25, 0:COLS] = own[7:8]
+        ref[f, 24:25, COLS : 2 * COLS] = jnp.where(lane < COLS // 2, to_the_e, to_the_w)[7:8]
 
     def window(first, reach):
         middle = first + REACH
@@ -560,13 +476,12 @@
     CHUNK = 24
     chunks = range(8, 8 + SPAN, CHUNK)
 
-    def tile_ready():
-        for start in chunks:
-            rows = slice(start, start + CHUNK)
-            seas = main_sides(X, 9, start, CHUNK)
-            surfaces = [X[5 + i, rows, :] + lap_of(seas, main_sides(X, 7 + i, start, CHUNK)) for i in range(2)]
-            ready(X, rows, slice(0, 2 * COLS), surfaces)
-            X[3, rows, :] = X[3, rows, :] * (RELAX / (1.0 + RELAX))
+    def chunk_ready(ref, start):
+        rows = slice(start, start + CHUNK)
+        seas = main_sides(ref, 9, start, CHUNK)
+        surfaces = [ref[5 + i, rows, :] + lap_of(seas, main_sides(ref, 7 + i, start, CHUNK)) for i in range(2)]
+        ready(ref, rows, slice(0, 2 * COLS), surfaces)
+        ref[3, rows, :] = ref[3, rows, :] * (RELAX / (1.0 + RELAX))
 
     def stress(u, v, third, old):
         twice_d = (u[1] - u[2]) + (v[3] - v[4])
@@ -588,90 +503,184 @@
 
     every = slice(0, 8)
 
-    def tile_stress(first):
+    def chunk_stress(vel, sig, start, first=False):
+        rows = slice(start, start + CHUNK)
+        u, v = main_sides(vel, 0, start, CHUNK), main_sides(vel, 1, start, CHUNK)
+        old = None if first else (sig[0, rows, :], sig[1, rows, :])
+        sig[0, rows, :], sig[1, rows, :] = stress(u, v, vel[3, rows, :], old)
+
+    def chunk_push(vel, sig, start):
+        a, b = main_sides(sig, 0, start, CHUNK), main_sides(sig, 1, start, CHUNK)
+        push(vel, vel, slice(start, start + CHUNK), slice(0, 2 * COLS), a, b)
+
+    def tile_cycle(cycle, carry):
         for start in chunks:
-            rows = slice(start, start + CHUNK)
-            u, v = main_sides(X, 0, start, CHUNK), main_sides(X, 1, start, CHUNK)
-            old = None if first else (AB[0, rows, :], AB[1, rows, :])
-            AB[0, rows, :], AB[1, rows, :] = stress(u, v, X[3, rows, :], old)
-
-    def tile_push():
+            chunk_stress(X, AB, start)
         for start in chunks:
-            rows = slice(start, start + CHUNK)
-            push(X, X, rows, slice(0, 2 * COLS), main_sides(AB, 0, start, CHUNK), main_sides(AB, 1, start, CHUNK))
-
-    def tile_cycle(cycle, carry):
-        tile_stress(False)
-        tile_push()
+            chunk_push(X, AB, start)
         return carry
+
+    low_piece, high_piece, low_tile, high_tile = slice(8, 16), slice(16, 24), slice(80, 88), slice(88, 96)
 
     def top_cycles(cycles):
         vel, sig, i_a, i_b = (S, SAB, 0, 1) if cycles[0] == 0 else (S2, S2, 2, 3)
         for cycle in cycles:
             left = 3 if cycle == cycles[0] else 1
-            close_top(X, 0, vel, 0, -1)
-            close_top(X, 1, vel, 1, -1)
+            close_top(XT, 0, vel, 0, -1)
+            close_top(XT, 1, vel, 1, -1)
             for win in windows(left):
                 cols = slice(COLS * win[0], COLS * win[1])
                 u, v = strip_sides(vel, 0, win, -1), strip_sides(vel, 1, win, -1)
                 old = (sig[i_a, :, cols], sig[i_b, :, cols]) if cycle else None
                 sig[i_a, :, cols], sig[i_b, :, cols] = stress(u, v, S[3, :, cols], old)
-            tile_stress(cycle == 0)
-            close_top(AB, 0, sig, i_a, 1)
-            close_top(AB, 1, sig, i_b, 1)
+            chunk_stress(XT, ABT, 8, cycle == 0)
+            close_top(ABT, 0, sig, i_a, 1)
+            close_top(ABT, 1, sig, i_b, 1)
             for win in windows(left - 1):
                 cols = slice(COLS * win[0], COLS * win[1])
                 push(S, vel, every, cols, strip_sides(sig, i_a, win, 1), strip_sides(sig, i_b, win, 1))
-            tile_push()
+            chunk_push(XT, ABT, 8)
 
     @pl.when(is_top)
     def _():
+        XT[...] = X[:, 72:112, :]
+        ABT[...] = jnp.zeros((2, 40, 2 * COLS), jnp.float32)
+
+    for start in chunks:
+        chunk_ready(X, start)
+    lax.fori_loop(0, 2, tile_cycle, 0)
+
+    @pl.when(is_top)
+    def _():
+        strips_arrive(False)
+        IDX[...] = jnp.broadcast_to(S[NF, 7:8, :], IDX.shape).astype(jnp.int32)
+        for f, sign in ((7, -1), (8, -1), (9, 1)):
+            close_top(XT, f, S, f, sign)
         strips_ready()
-        tile_ready()
+        chunk_ready(XT, 8)
         top_cycles((0, 1))
-        SS2[0:2] = X[0:2, last8, 0:COLS]
-        SS2[2:4] = AB[:, last8, 0:COLS]
+        SS2[0:2] = XT[0:2, high_piece, 0:COLS]
+        SS2[2:4] = ABT[:, high_piece, 0:COLS]
+        strips_start(True)
         S2[:, :, middle] = SS2[...]
-        strips_start(True)
+        X[0:2, high_tile, :] = XT[0:2, high_piece, :]
+        X[5:7, high_tile, :] = XT[5:7, high_piece, :]
+        AB[:, high_tile, :] = ABT[:, high_piece, :]
+        XT[0:2, low_piece, :] = X[0:2, low_tile, :]
+        ABT[:, low_piece, :] = AB[:, low_tile, :]
+
+    lax.fori_loop(0, 2, tile_cycle, 0)
+
+    away = pl.ds(pl.multiple_of(TOP + HALF * (1 - comp), 8), HALF)
+    here = pl.ds(pl.multiple_of(TOP + HALF * comp, 8), HALF)
+    ice_out = (new_ice_u, new_ice_v)
+    vel_away = [
+        send(X.at[i, away, 0:COLS], ice_out[i].at[:, mine], vel_send.at[i], vel_recv.at[i], partner) for i in range(2)
+    ]
+    vel_here = [
+        pltpu.make_async_copy(X.at[i, here, 0:COLS], ice_out[i].at[:, mine], out_sem.at[3 + i]) for i in range(2)
+    ]
 
     @pl.when(jnp.logical_not(is_top))
     def _():
-        tile_ready()
-        AB[:, 8 : 8 + SPAN, :] = jnp.zeros((2, SPAN, 2 * COLS), jnp.float32)
-        lax.fori_loop(0, 2, tile_cycle, 0)
-
-    regrid(0)
-    stores = [store(0)]
-    regrid(1)
+        for copy in vel_away + vel_here:
+            copy.start()
+
+    col_to_e.wait()
+    col_to_w.wait()
+
+    @pl.when(has_north)
+    def _():
+        row_n.wait_send()
+        row_s.wait_recv()
+
+    @pl.when(has_south)
+    def _():
+        row_s.wait_send()
+        row_n.wait_recv()
+
+
+    @pl.when(is_top)
+    def _():
+        row_f.wait()
+        inside = jnp.broadcast_to(fold_partner[...] - COLS * mirror, (8, COLS))
+
+        def fold_edge(f, carry):
+            taken = jnp.take_along_axis(F[f, 88:96, :], inside, axis=1, mode="promise_in_bounds")
+            F[f, 88:96, :] = jnp.where((f < LEV) | (f == 3 * LEV), taken, -taken)
+            return carry
+
+        lax.fori_loop(0, PLANES, fold_edge, 0, unroll=7)
+
+    GE[...] = jnp.where((lane & 1) == 0, pltpu.roll(RE[...], COLS - 1, 1), pltpu.roll(RW[...], 1, 1))
+
+    def plane_sides(f):
+        value = F[f, 8 : 8 + ROWS, :]
+        edges = pltpu.roll(GE[...], COLS - 1 - 2 * f, 1)
+        to_east = jnp.where(lane == COLS - 1, edges, pltpu.roll(value, COLS - 1, 1))
+        to_west = jnp.where(lane == 0, edges, pltpu.roll(value, 1, 1))
+        return value, to_east, to_west, F[f, 9 : 9 + ROWS, :], F[f, 7 : 7 + ROWS, :]
+
+    seas = plane_sides(3 * LEV)
+    degree = jnp.zeros((ROWS, COLS), jnp.float32)
+    for i in range(4):
+        weight = seas[0] * seas[i + 1]
+        MK[i] = weight
+        degree = degree + weight
+    MK[4] = degree
+
+    def diffuse(g):
+        coefficient = diffusivity if g == 0 else viscosity
+
+        def one(l, carry):
+            f = g * LEV + l
+            value, to_east, to_west, to_north, to_south = plane_sides(f)
+            total = MK[0] * to_east + MK[1] * to_west + MK[2] * to_north + MK[3] * to_south
+            new = value + coefficient[l] * (total - MK[4] * value)
+            high = new.astype(jnp.bfloat16)
+            DH[f] = high
+            DL[f] = (new - high.astype(jnp.float32)).astype(jnp.bfloat16)
+            return carry
+
+        lax.fori_loop(0, LEV, one, 0, unroll=4)
+
+    def regrid(g):
+        planes = slice(g * LEV, (g + 1) * LEV)
+        pieces = range(0, ROWS, LEV)
+        high = jnp.concatenate([DH[planes, r : r + LEV, :].reshape(LEV * LEV, COLS) for r in pieces], axis=1)
+        low = jnp.concatenate([DL[planes, r : r + LEV, :].reshape(LEV * LEV, COLS) for r in pieces], axis=1)
+        new = jnp.dot(KK[...], jnp.concatenate([high, high, low], axis=0), preferred_element_type=jnp.float32)
+        for i, r in enumerate(pieces):
+            O[planes, r : r + LEV, :] = new[:, COLS * i : COLS * (i + 1)].reshape(LEV, LEV, COLS)
+
+    outs = (new_tracer, new_ocean_u, new_ocean_v)
+
+    def store(g):
+        copy = pltpu.make_async_copy(O.at[g * LEV : (g + 1) * LEV], outs[g], out_sem.at[g])
+        copy.start()
+        return copy
+
+    diffuse(0)
+    diffuse(1)
 
     @pl.when(is_top)
     def _():
         strips_arrive(True)
         to_the_e = S2[0:2, 7:8, COLS * (REACH + 1) : COLS * (REACH + 2)]
         to_the_w = S2[0:2, 7:8, COLS * (REACH - 1) : COLS * REACH]
-        X[0:2, TOP + ROWS - 1 : TOP + ROWS, COLS : 2 * COLS] = jnp.where(lane < COLS // 2, to_the_e, to_the_w)
+        XT[0:2, 23:24, COLS : 2 * COLS] = jnp.where(lane < COLS // 2, to_the_e, to_the_w)
         top_cycles((2, 3))
-
-    @pl.when(jnp.logical_not(is_top))
-    def _():
-        lax.fori_loop(0, 2, tile_cycle, 0)
-
-    away = pl.ds(pl.multiple_of(TOP + HALF * (1 - comp), 8), HALF)
-    here = pl.ds(pl.multiple_of(TOP + HALF * comp, 8), HALF)
-    ice_out = (new_ice_u, new_ice_v)
-    vel_away, vel_here = [], []
-    for i in range(2):
-        copy = send(X.at[i, away, 0:COLS], ice_out[i].at[:, mine], vel_send.at[i], vel_recv.at[i], partner)
-        copy.start()
-        vel_away.append(copy)
-        copy = pltpu.make_async_copy(X.at[i, here, 0:COLS], ice_out[i].at[:, mine], out_sem.at[3 + i])
-        copy.start()
-        vel_here.append(copy)
+        X[0:2, high_tile, :] = XT[0:2, high_piece, :]
+        for copy in vel_away + vel_here:
+            copy.start()
+
+    diffuse(2)
+    regrid(0)
+    stores = [store(0)]
 
     for i in range(2):
         g = i + 1
-        if g == 2:
-            regrid(g)
+        regrid(g)
         tau = X[i, tile_rows, 0:COLS] - X[5 + i, tile_rows, 0:COLS] * (1.0 / SHARE)
         O[g * LEV] = O[g * LEV] + COUPLE * (X[9, tile_rows, 0:COLS] * tau)
         stores.append(store(g))
@@ -734,6 +743,8 @@
                 vmem((3 * LEV, ROWS, COLS), f32),
                 vmem((NF, 112, 2 * COLS), f32),
                 vmem((2, 112, 2 * COLS), f32),
+                vmem((NF, 40, 2 * COLS), f32),
+                vmem((2, 40, 2 * COLS), f32),
                 vmem((NS, 8, BLOCKS * COLS), f32),
                 vmem((2, 8, BLOCKS * COLS), f32),
                 vmem((NS, 8, COLS), f32),

time: 28.2 us -> 29 us (1.028)
  Pallas kernels: 27.5 us -> 28.2 us
    pallas_call x1, Pallas kernels: 26.2 us -> 26.9 us  [body(): pl.pallas_call(step, out_shape=shapes, in_specs=[main_memory] * 13, out_s...]
where the time goes in v1:
time: 29 us; the launch traced here: 28.9 us
  Pallas kernels  28.2 us (97%)
  between operations  0.64 us (2%)
    pallas_call x1, Pallas kernels, body(): pl.pallas_call(step, out_shape=shapes, in_specs=[main_memory] * 13, out_s...  26.9 us
    pallas_call x1, Pallas kernels, body(): pl.pallas_call(deliver, out_shape=shapes, in_specs=[anywhere] * 5, out_sp...  1.32 us

profile of v1, /device:TPU:224, one launch (start us, length us, event | category | flops | bytes accessed | tf_op | source)
XLA Modules:
  0.0 28.9 jit_solution(10954095587955135593)
XLA Ops:
  0.6 26.9 %shard_map.164 = (f32[16,80,128]{2,1,0:T(8,128)S(1)}, f32[16,80,128]{2,1,0:T(8,128)S(1)}, f32[16,80,128]{2,1,0:T(8,128)S(1)}, f32[40,256]{1,0:T(8,128)S(1)}, f32[40,256]{1,0:T(8,128)S(1)}) custom-call(f32[16,80,128]{2,1,0:T(8,128)} %args_0_.4, f32[16,80,128]{2,1,0:T(8,128)} %args_1_.4, f32[16,80,128]{2,1,0:T(8,128)} %args_2_.4, s32[80,128]{1,0:T(8,128)} %args_3_.4, ...), custom_call_target="tpu_custom_call" | custom-call | tf_op jit(solution)/shard_map/pallas_call | solution.py:733
  27.5 1.3 %shard_map.165 = (f32[16,80,128]{2,1,0:T(8,128)}, f32[16,80,128]{2,1,0:T(8,128)}, f32[16,80,128]{2,1,0:T(8,128)}, f32[40,256]{1,0:T(8,128)}, f32[40,256]{1,0:T(8,128)}) custom-call(f32[16,80,128]{2,1,0:T(8,128)S(1)} %get-tuple-element.10.refs_0_, f32[16,80,128]{2,1,0:T(8,128)S(1)} %get-tuple-element.11.refs_1_, ...), custom_call_target="tpu_custom_call" | custom-call | tf_op jit(solution)/shard_map/pallas_call | solution.py:805

commit v2 on v1

--- a/solution.py
+++ b/solution.py
@@ -15,7 +15,7 @@
 ROWS = 80
 HALF = 40
 COLS = 128
-NF = 10
+NF = 7
 NS = NF + 1
 REACH = 2
 SIDE = 2 * REACH + 1
@@ -26,7 +26,8 @@
 MIRROR_REACH = {1: 0, 2: 1, 3: 2}
 OWN_ROWS = (8, 2, 1)
 MIRROR_ROWS = (4, 3, 2)
-PLANES = 3 * LEV + 1
+SEA = 3 * LEV
+PLANES = SEA + 3
 
 
 def kernel(
@@ -68,7 +69,12 @@
     PW,
     EB,
     WB,
-    CP,
+    EBS,
+    WBS,
+    EBN,
+    WBN,
+    CE,
+    CW,
     RE,
     RW,
     GE,
@@ -180,15 +186,15 @@
     @pl.when(jnp.logical_not(has_south))
     def _():
         X[:, south8, 0:COLS] = jnp.zeros((NF, 8, COLS), jnp.float32)
-        EB[0:8, :] = jnp.zeros((8, COLS), jnp.float32)
-        WB[0:8, :] = jnp.zeros((8, COLS), jnp.float32)
+        EBS[...] = jnp.zeros((8, COLS), jnp.float32)
+        WBS[...] = jnp.zeros((8, COLS), jnp.float32)
         F[:, 0:8, :] = jnp.zeros((PLANES, 8, COLS), jnp.float32)
 
     @pl.when(is_top)
     def _():
         X[:, north8, 0:COLS] = jnp.zeros((NF, 8, COLS), jnp.float32)
-        EB[88:96, :] = jnp.zeros((8, COLS), jnp.float32)
-        WB[88:96, :] = jnp.zeros((8, COLS), jnp.float32)
+        EBN[...] = jnp.zeros((8, COLS), jnp.float32)
+        WBN[...] = jnp.zeros((8, COLS), jnp.float32)
 
     outer = jnp.zeros((NF, 8, 2 * COLS), jnp.float32)
     X[:, 0:8, :] = outer
@@ -228,18 +234,18 @@
     for copy in small:
         copy.wait()
     sea = OM[...].astype(jnp.float32)
-    X[9, tile_rows, 0:COLS] = sea
-    F[3 * LEV, 8 : 8 + ROWS, :] = sea
+    F[SEA, 8 : 8 + ROWS, :] = sea
     for i, copy in ((0, load_u), (1, load_v)):
         copy.wait()
-        base = jnp.zeros((ROWS, COLS), jnp.float32)
-        spread = jnp.zeros((ROWS, COLS), jnp.float32)
-        for l in range(LEV):
+
+        def level(l, sums, i=i):
             weighted = remap[0, l] * F[LEV * (i + 1) + l, 8 : 8 + ROWS, :]
-            base = base + weighted
-            spread = spread + viscosity[l] * weighted
+            return sums[0] + weighted, sums[1] + viscosity[l] * weighted
+
+        zero = jnp.zeros((ROWS, COLS), jnp.float32)
+        base, spread = lax.fori_loop(0, LEV, level, (zero, zero), unroll=4)
         X[5 + i, tile_rows, 0:COLS] = base
-        X[7 + i, tile_rows, 0:COLS] = spread
+        F[SEA + 1 + i, 8 : 8 + ROWS, :] = spread
 
     load_t.wait()
     row_n = send(F.at[:, 87:88, :], F.at[:, 7:8, :], edge_send.at[2], edge_recv.at[2], at(me, gy + 1))
@@ -261,9 +267,12 @@
     def pack(f, packed):
         return jnp.where((lane >> 1) == f, pltpu.roll(F[f, 8 : 8 + ROWS, :], 2 * f + 1, 1), packed)
 
-    CP[...] = lax.fori_loop(0, PLANES, pack, jnp.zeros((ROWS, COLS), jnp.float32), unroll=7)
-    col_to_e = send(CP, RW, edge_send.at[0], edge_recv.at[0], at(east, gy))
-    col_to_w = send(CP, RE, edge_send.at[1], edge_recv.at[1], at(west, gy))
+    packed = lax.fori_loop(0, PLANES, pack, jnp.zeros((ROWS, COLS), jnp.float32), unroll=3)
+    even = (lane & 1) == 0
+    CE[...] = jnp.where(even, packed[0:HALF], pltpu.roll(packed[HALF:ROWS], 1, 1))
+    CW[...] = jnp.where(even, pltpu.roll(packed[HALF:ROWS], COLS - 1, 1), packed[0:HALF])
+    col_to_e = send(CE, RW, edge_send.at[0], edge_recv.at[0], at(east, gy))
+    col_to_w = send(CW, RE, edge_send.at[1], edge_recv.at[1], at(west, gy))
     col_to_e.start()
     col_to_w.start()
 
@@ -281,31 +290,85 @@
         KK[rows, 256:512] = jnp.where(diagonal, low[k : k + 1], 0.0).astype(jnp.bfloat16)
         KK[rows, 512:768] = high_k
 
+    col_to_e.wait()
+    col_to_w.wait()
+
+    @pl.when(has_north)
+    def _():
+        row_n.wait_send()
+        row_s.wait_recv()
+
+    @pl.when(has_south)
+    def _():
+        row_s.wait_send()
+        row_n.wait_recv()
+
+
+    @pl.when(is_top)
+    def _():
+        row_f.wait()
+        inside = jnp.broadcast_to(fold_partner[...] - COLS * mirror, (8, COLS))
+
+        for f in range(SEA, PLANES):
+            taken = jnp.take_along_axis(F[f, 88:96, :], inside, axis=1, mode="promise_in_bounds")
+            F[f, 88:96, :] = taken if f == SEA else -taken
+
+    GE[0:HALF] = jnp.where(even, pltpu.roll(RE[...], COLS - 1, 1), pltpu.roll(RW[...], 1, 1))
+    GE[HALF:ROWS] = jnp.where(even, RE[...], RW[...])
+
+    def plane_sides(f):
+        value = F[f, 8 : 8 + ROWS, :]
+        edges = pltpu.roll(GE[...], COLS - 1 - 2 * f, 1)
+        to_east = jnp.where(lane == COLS - 1, edges, pltpu.roll(value, COLS - 1, 1))
+        to_west = jnp.where(lane == 0, edges, pltpu.roll(value, 1, 1))
+        return value, to_east, to_west, F[f, 9 : 9 + ROWS, :], F[f, 7 : 7 + ROWS, :]
+
+    seas = plane_sides(SEA)
+    degree = jnp.zeros((ROWS, COLS), jnp.float32)
+    for i in range(4):
+        weight = seas[0] * seas[i + 1]
+        MK[i] = weight
+        degree = degree + weight
+    MK[4] = degree
+
+    def lap(f):
+        value, to_east, to_west, to_north, to_south = plane_sides(f)
+        total = MK[0] * to_east + MK[1] * to_west + MK[2] * to_north + MK[3] * to_south
+        return value, total - MK[4] * value
+
+    for i in range(2):
+        X[5 + i, tile_rows, 0:COLS] = X[5 + i, tile_rows, 0:COLS] + lap(SEA + 1 + i)[1]
+
     for i in range(5):
         ice_local[i].wait()
         ice_away[i].wait_recv()
     X[4, tile_rows, 0:COLS] = IM[...].astype(jnp.float32)
 
-    pack_e = jnp.zeros((ROWS, COLS), jnp.float32)
-    pack_w = jnp.zeros((ROWS, COLS), jnp.float32)
-    for f in range(NF):
-        value = X[f, tile_rows, 0:COLS]
-        keep = (lane >= 8 * f) & (lane < 8 * f + 8)
-        pack_e = jnp.where(keep, pltpu.roll(value, 8 * f + 8, 1), pack_e)
-        pack_w = jnp.where(keep, pltpu.roll(value, 8 * f, 1) if f else value, pack_w)
+
+    def rim_pack(f, packed):
+        south_half, north_half = X[f, TOP : TOP + HALF, 0:COLS], X[f, TOP + HALF : TOP + ROWS, 0:COLS]
+        group = lane >> 3
+        new = []
+        for edge, old in ((8, packed[0]), (0, packed[1])):
+            kept = jnp.where(group == f, pltpu.roll(south_half, 8 * f + edge, 1), old)
+            new.append(jnp.where(group == f + 8, pltpu.roll(north_half, 64 + 8 * f + edge, 1), kept))
+        return tuple(new)
+
+    zero = jnp.zeros((HALF, COLS), jnp.float32)
+    pack_e, pack_w = lax.fori_loop(0, NF, rim_pack, (zero, zero), unroll=7)
     PE[...] = pack_e
     PW[...] = pack_w
-    to_e = send(PE, WB.at[8 : 8 + ROWS], rim_send.at[0], rim_recv.at[0], at(east, gy))
-    to_w = send(PW, EB.at[8 : 8 + ROWS], rim_send.at[1], rim_recv.at[1], at(west, gy))
+    to_e = send(PE, WB, rim_send.at[0], rim_recv.at[0], at(east, gy))
+    to_w = send(PW, EB, rim_send.at[1], rim_recv.at[1], at(west, gy))
     to_n = [
         send(X.at[:, last8, 0:COLS], X.at[:, south8, 0:COLS], rim_send.at[2], rim_recv.at[2], at(me, gy + 1)),
-        send(PE.at[ROWS - 8 : ROWS], WB.at[0:8], rim_send.at[3], rim_recv.at[3], at(east, gy + 1)),
-        send(PW.at[ROWS - 8 : ROWS], EB.at[0:8], rim_send.at[4], rim_recv.at[4], at(west, gy + 1)),
+        send(PE.at[HALF - 8 : HALF], WBS, rim_send.at[3], rim_recv.at[3], at(east, gy + 1)),
+        send(PW.at[HALF - 8 : HALF], EBS, rim_send.at[4], rim_recv.at[4], at(west, gy + 1)),
     ]
     to_s = [
         send(X.at[:, first8, 0:COLS], X.at[:, north8, 0:COLS], rim_send.at[5], rim_recv.at[5], at(me, gy - 1)),
-        send(PE.at[0:8], WB.at[88:96], rim_send.at[6], rim_recv.at[6], at(east, gy - 1)),
-        send(PW.at[0:8], EB.at[88:96], rim_send.at[7], rim_recv.at[7], at(west, gy - 1)),
+        send(PE.at[0:8], WBN, rim_send.at[6], rim_recv.at[6], at(east, gy - 1)),
+        send(PW.at[0:8], EBN, rim_send.at[7], rim_recv.at[7], at(west, gy - 1)),
     ]
 
     def strip_ends(src, dst, slot, rows):
@@ -369,6 +432,28 @@
         S[:, :, middle] = SS[...]
         strips_start(False)
 
+    def diffuse(f, carry):
+        coefficient = jnp.where(f < LEV, diffusivity[f & (LEV - 1)], viscosity[f & (LEV - 1)])
+        value, spread = lap(f)
+        new = value + coefficient * spread
+        high = new.astype(jnp.bfloat16)
+        DH[f] = high
+        DL[f] = (new - high.astype(jnp.float32)).astype(jnp.bfloat16)
+        return carry
+
+    @pl.when(is_top)
+    def _():
+        inside = jnp.broadcast_to(fold_partner[...] - COLS * mirror, (8, COLS))
+
+        def fold_edge(f, carry):
+            taken = jnp.take_along_axis(F[f, 88:96, :], inside, axis=1, mode="promise_in_bounds")
+            F[f, 88:96, :] = jnp.where(f < LEV, taken, -taken)
+            return carry
+
+        lax.fori_loop(0, 3 * LEV, fold_edge, 0, unroll=8)
+
+    lax.fori_loop(0, 3 * LEV, diffuse, 0, unroll=4)
+
     to_e.wait()
     to_w.wait()
 
@@ -386,12 +471,21 @@
         for copy in to_n:
             copy.wait_recv()
 
-    for f in range(NF):
-        from_e = pltpu.roll(EB[...], COLS - 8 * f, 1) if f else EB[...]
-        from_w = pltpu.roll(WB[...], COLS - 8 - 8 * f, 1)
-        X[f, 8 : 8 + SPAN, COLS : 2 * COLS] = jnp.where(
-            lane < 8, from_e, jnp.where(lane >= COLS - 8, from_w, 0.0)
-        )
+    def rim_unpack(f, carry):
+        def put(rows, e, w, half):
+            from_e = pltpu.roll(e, lax.rem(COLS + half - 8 * f, COLS), 1)
+            from_w = pltpu.roll(w, lax.rem(2 * COLS - 8 + half - 8 * f, COLS), 1)
+            X[f, rows, COLS : 2 * COLS] = jnp.where(
+                lane < 8, from_e, jnp.where(lane >= COLS - 8, from_w, 0.0)
+            )
+
+        put(slice(TOP, TOP + HALF), EB[...], WB[...], 0)
+        put(slice(TOP + HALF, TOP + ROWS), EB[...], WB[...], 64)
+        put(slice(TOP - 8, TOP), EBS[...], WBS[...], 64)
+        put(slice(TOP + ROWS, TOP + ROWS + 8), EBN[...], WBN[...], 0)
+        return carry
+
+    lax.fori_loop(0, NF, rim_unpack, 0, unroll=7)
 
     def inside_of(i):
         return IDX[:, COLS * i : COLS * (i + 1)]
@@ -436,32 +530,17 @@
             found.append(window(SIDE, MIRROR_REACH[left]))
         return found
 
-    def lap_of(seas, values):
-        total = seas[1] * (values[1] - values[0])
-        for i in range(2, 5):
-            total = total + seas[i] * (values[i] - values[0])
-        return total * seas[0]
-
     SHARE = STEP_SIZE / (1.0 + STEP_SIZE)
     KEEP = 1.0 / (1.0 + STEP_SIZE)
 
-    def ready(ref, rows, cols, surfaces):
+    def ready(ref, rows, cols):
         present = ref[4, rows, cols]
-        ref[5, rows, cols] = SHARE * present * surfaces[0]
-        ref[6, rows, cols] = SHARE * present * surfaces[1]
+        ref[5, rows, cols] = SHARE * present * ref[5, rows, cols]
+        ref[6, rows, cols] = SHARE * present * ref[6, rows, cols]
         mass = ref[2, rows, cols]
         ref[2, rows, cols] = 0.5 * SHARE * present / jnp.where(mass > 0.0, mass, 1.0)
         ref[4, rows, cols] = KEEP * present
-
-    def strips_ready():
-        for win in windows(2):
-            cols = slice(COLS * win[0], COLS * win[1])
-            seas = strip_sides(S, 9, win, 1)
-            surfaces = [
-                S[5 + i, :, cols] + lap_of(seas, strip_sides(S, 7 + i, win, -1)) for i in range(2)
-            ]
-            ready(S, slice(0, 8), cols, surfaces)
-        S[3] = S[3] * (RELAX / (1.0 + RELAX))
+        ref[3, rows, cols] = ref[3, rows, cols] * (RELAX / (1.0 + RELAX))
 
     def main_sides(ref, f, start, size):
         value = ref[f, start : start + size, :]
@@ -475,13 +554,6 @@
 
     CHUNK = 24
     chunks = range(8, 8 + SPAN, CHUNK)
-
-    def chunk_ready(ref, start):
-        rows = slice(start, start + CHUNK)
-        seas = main_sides(ref, 9, start, CHUNK)
-        surfaces = [ref[5 + i, rows, :] + lap_of(seas, main_sides(ref, 7 + i, start, CHUNK)) for i in range(2)]
-        ready(ref, rows, slice(0, 2 * COLS), surfaces)
-        ref[3, rows, :] = ref[3, rows, :] * (RELAX / (1.0 + RELAX))
 
     def stress(u, v, third, old):
         twice_d = (u[1] - u[2]) + (v[3] - v[4])
@@ -541,30 +613,27 @@
                 push(S, vel, every, cols, strip_sides(sig, i_a, win, 1), strip_sides(sig, i_b, win, 1))
             chunk_push(XT, ABT, 8)
 
+    for start in chunks:
+        ready(X, slice(start, start + CHUNK), slice(0, 2 * COLS))
+
     @pl.when(is_top)
     def _():
         XT[...] = X[:, 72:112, :]
         ABT[...] = jnp.zeros((2, 40, 2 * COLS), jnp.float32)
 
-    for start in chunks:
-        chunk_ready(X, start)
     lax.fori_loop(0, 2, tile_cycle, 0)
 
     @pl.when(is_top)
     def _():
         strips_arrive(False)
         IDX[...] = jnp.broadcast_to(S[NF, 7:8, :], IDX.shape).astype(jnp.int32)
-        for f, sign in ((7, -1), (8, -1), (9, 1)):
-            close_top(XT, f, S, f, sign)
-        strips_ready()
-        chunk_ready(XT, 8)
+        ready(S, every, slice(0, BLOCKS * COLS))
         top_cycles((0, 1))
         SS2[0:2] = XT[0:2, high_piece, 0:COLS]
         SS2[2:4] = ABT[:, high_piece, 0:COLS]
         strips_start(True)
         S2[:, :, middle] = SS2[...]
         X[0:2, high_tile, :] = XT[0:2, high_piece, :]
-        X[5:7, high_tile, :] = XT[5:7, high_piece, :]
         AB[:, high_tile, :] = ABT[:, high_piece, :]
         XT[0:2, low_piece, :] = X[0:2, low_tile, :]
         ABT[:, low_piece, :] = AB[:, low_tile, :]
@@ -586,66 +655,8 @@
         for copy in vel_away + vel_here:
             copy.start()
 
-    col_to_e.wait()
-    col_to_w.wait()
-
-    @pl.when(has_north)
-    def _():
-        row_n.wait_send()
-        row_s.wait_recv()
-
-    @pl.when(has_south)
-    def _():
-        row_s.wait_send()
-        row_n.wait_recv()
-
-
-    @pl.when(is_top)
-    def _():
-        row_f.wait()
-        inside = jnp.broadcast_to(fold_partner[...] - COLS * mirror, (8, COLS))
-
-        def fold_edge(f, carry):
-            taken = jnp.take_along_axis(F[f, 88:96, :], inside, axis=1, mode="promise_in_bounds")
-            F[f, 88:96, :] = jnp.where((f < LEV) | (f == 3 * LEV), taken, -taken)
-            return carry
-
-        lax.fori_loop(0, PLANES, fold_edge, 0, unroll=7)
-
-    GE[...] = jnp.where((lane & 1) == 0, pltpu.roll(RE[...], COLS - 1, 1), pltpu.roll(RW[...], 1, 1))
-
-    def plane_sides(f):
-        value = F[f, 8 : 8 + ROWS, :]
-        edges = pltpu.roll(GE[...], COLS - 1 - 2 * f, 1)
-        to_east = jnp.where(lane == COLS - 1, edges, pltpu.roll(value, COLS - 1, 1))
-        to_west = jnp.where(lane == 0, edges, pltpu.roll(value, 1, 1))
-        return value, to_east, to_west, F[f, 9 : 9 + ROWS, :], F[f, 7 : 7 + ROWS, :]
-
-    seas = plane_sides(3 * LEV)
-    degree = jnp.zeros((ROWS, COLS), jnp.float32)
-    for i in range(4):
-        weight = seas[0] * seas[i + 1]
-        MK[i] = weight
-        degree = degree + weight
-    MK[4] = degree
-
-    def diffuse(g):
-        coefficient = diffusivity if g == 0 else viscosity
-
-        def one(l, carry):
-            f = g * LEV + l
-            value, to_east, to_west, to_north, to_south = plane_sides(f)
-            total = MK[0] * to_east + MK[1] * to_west + MK[2] * to_north + MK[3] * to_south
-            new = value + coefficient[l] * (total - MK[4] * value)
-            high = new.astype(jnp.bfloat16)
-            DH[f] = high
-            DL[f] = (new - high.astype(jnp.float32)).astype(jnp.bfloat16)
-            return carry
-
-        lax.fori_loop(0, LEV, one, 0, unroll=4)
-
     def regrid(g):
-        planes = slice(g * LEV, (g + 1) * LEV)
+        planes = pl.ds(g * LEV, LEV)
         pieces = range(0, ROWS, LEV)
         high = jnp.concatenate([DH[planes, r : r + LEV, :].reshape(LEV * LEV, COLS) for r in pieces], axis=1)
         low = jnp.concatenate([DL[planes, r : r + LEV, :].reshape(LEV * LEV, COLS) for r in pieces], axis=1)
@@ -653,18 +664,13 @@
         for i, r in enumerate(pieces):
             O[planes, r : r + LEV, :] = new[:, COLS * i : COLS * (i + 1)].reshape(LEV, LEV, COLS)
 
-    outs = (new_tracer, new_ocean_u, new_ocean_v)
-
-    def store(g):
-        copy = pltpu.make_async_copy(O.at[g * LEV : (g + 1) * LEV], outs[g], out_sem.at[g])
-        copy.start()
-        return copy
-
-    diffuse(0)
-    diffuse(1)
-
-    @pl.when(is_top)
-    def _():
+    @pl.when(is_top)
+    def _():
+        def early(g, carry):
+            regrid(g)
+            return carry
+
+        lax.fori_loop(0, 2, early, 0)
         strips_arrive(True)
         to_the_e = S2[0:2, 7:8, COLS * (REACH + 1) : COLS * (REACH + 2)]
         to_the_w = S2[0:2, 7:8, COLS * (REACH - 1) : COLS * REACH]
@@ -674,16 +680,29 @@
         for copy in vel_away + vel_here:
             copy.start()
 
-    diffuse(2)
-    regrid(0)
-    stores = [store(0)]
-
-    for i in range(2):
-        g = i + 1
-        regrid(g)
-        tau = X[i, tile_rows, 0:COLS] - X[5 + i, tile_rows, 0:COLS] * (1.0 / SHARE)
-        O[g * LEV] = O[g * LEV] + COUPLE * (X[9, tile_rows, 0:COLS] * tau)
-        stores.append(store(g))
+    outs = (new_tracer, new_ocean_u, new_ocean_v)
+
+    stores = [
+        pltpu.make_async_copy(O.at[g * LEV : (g + 1) * LEV], outs[g], out_sem.at[g]) for g in range(3)
+    ]
+
+    def finish(g, carry):
+        @pl.when(jnp.logical_not(is_top) | (g == 2))
+        def _():
+            regrid(g)
+
+        for i in range(3):
+
+            @pl.when(g == i)
+            def _(i=i):
+                if i:
+                    tau = X[i - 1, tile_rows, 0:COLS] - X[4 + i, tile_rows, 0:COLS] * (1.0 / SHARE)
+                    O[i * LEV] = O[i * LEV] + COUPLE * (F[SEA, 8 : 8 + ROWS, :] * tau)
+                stores[i].start()
+
+        return carry
+
+    lax.fori_loop(0, 3, finish, 0)
 
     @pl.when(is_top)
     def _():
@@ -750,13 +769,18 @@
                 vmem((NS, 8, COLS), f32),
                 vmem((4, 8, BLOCKS * COLS), f32),
                 vmem((4, 8, COLS), f32),
-                vmem((ROWS, COLS), f32),
-                vmem((ROWS, COLS), f32),
-                vmem((SPAN, COLS), f32),
-                vmem((SPAN, COLS), f32),
-                vmem((ROWS, COLS), f32),
-                vmem((ROWS, COLS), f32),
-                vmem((ROWS, COLS), f32),
+                vmem((HALF, COLS), f32),
+                vmem((HALF, COLS), f32),
+                vmem((HALF, COLS), f32),
+                vmem((HALF, COLS), f32),
+                vmem((8, COLS), f32),
+                vmem((8, COLS), f32),
+                vmem((8, COLS), f32),
+                vmem((8, COLS), f32),
+                vmem((HALF, COLS), f32),
+                vmem((HALF, COLS), f32),
+                vmem((HALF, COLS), f32),
+                vmem((HALF, COLS), f32),
                 vmem((ROWS, COLS), f32),
                 vmem((5, ROWS, COLS), f32),
                 vmem((ROWS, COLS), jnp.int32),

time: 29 us -> 28.6 us (0.986)
  Pallas kernels: 28.2 us -> 27.8 us
    pallas_call x1, Pallas kernels: 26.9 us -> 26.5 us  [body(): pl.pallas_call(step, out_shape=shapes, in_specs=[main_memory] * 13, out_s...]
where the time goes in v2:
time: 28.6 us; the launch traced here: 28.5 us
  Pallas kernels  27.8 us (97%)
  between operations  0.64 us (2%)
    pallas_call x1, Pallas kernels, body(): pl.pallas_call(step, out_shape=shapes, in_specs=[main_memory] * 13, out_s...  26.5 us
    pallas_call x1, Pallas kernels, body(): pl.pallas_call(deliver, out_shape=shapes, in_specs=[anywhere] * 5, out_sp...  1.32 us

profile of v2, /device:TPU:224, one launch (start us, length us, event | category | flops | bytes accessed | tf_op | source)
XLA Modules:
  0.0 28.5 jit_solution(11204038640000193350)
XLA Ops:
  0.6 26.5 %shard_map.164 = (f32[16,80,128]{2,1,0:T(8,128)S(1)}, f32[16,80,128]{2,1,0:T(8,128)S(1)}, f32[16,80,128]{2,1,0:T(8,128)S(1)}, f32[40,256]{1,0:T(8,128)S(1)}, f32[40,256]{1,0:T(8,128)S(1)}) custom-call(f32[16,80,128]{2,1,0:T(8,128)} %args_0_.4, f32[16,80,128]{2,1,0:T(8,128)} %args_1_.4, f32[16,80,128]{2,1,0:T(8,128)} %args_2_.4, s32[80,128]{1,0:T(8,128)} %args_3_.4, ...), custom_call_target="tpu_custom_call" | custom-call | tf_op jit(solution)/shard_map/pallas_call | solution.py:752
  27.1 1.3 %shard_map.165 = (f32[16,80,128]{2,1,0:T(8,128)}, f32[16,80,128]{2,1,0:T(8,128)}, f32[16,80,128]{2,1,0:T(8,128)}, f32[40,256]{1,0:T(8,128)}, f32[40,256]{1,0:T(8,128)}) custom-call(f32[16,80,128]{2,1,0:T(8,128)S(1)} %get-tuple-element.10.refs_0_, f32[16,80,128]{2,1,0:T(8,128)S(1)} %get-tuple-element.11.refs_1_, ...), custom_call_target="tpu_custom_call" | custom-call | tf_op jit(solution)/shard_map/pallas_call | solution.py:829

commit v3 on v2

--- a/solution.py
+++ b/solution.py
@@ -28,6 +28,9 @@
 MIRROR_ROWS = (4, 3, 2)
 SEA = 3 * LEV
 PLANES = SEA + 3
+
+
+quarters = [slice(4 * i, 4 * i + 4) for i in range(LEV // 4)]
 
 
 def kernel(
@@ -73,6 +76,18 @@
     WBS,
     EBN,
     WBN,
+    TR,
+    BR,
+    NR,
+    SR,
+    CK,
+    RKE,
+    RKW,
+    GK,
+    TK,
+    BK,
+    NK,
+    SK,
     CE,
     CW,
     RE,
@@ -93,6 +108,8 @@
     ice_recv,
     edge_send,
     edge_recv,
+    first_send,
+    first_recv,
     rim_send,
     rim_recv,
     strip_send,
@@ -123,43 +140,18 @@
         strips.append((SIDE + REACH + d, wrap(mirror + d), d % 2 == 1, MIRROR_ROWS[abs(d)]))
         strips.append((REACH + d, wrap(me - d), False, OWN_ROWS[abs(d)]))
 
-    barrier = pltpu.get_barrier_semaphore()
-
-    def greet(target):
-        pl.semaphore_signal(barrier, inc=1, device_id=target, device_id_type=MESH)
-
-    greet(at(east, gy))
-    greet(at(west, gy))
-
-    @pl.when(has_north)
-    def _():
-        for block in (me, east, west):
-            greet(at(block, gy + 1))
-
-    @pl.when(has_south)
-    def _():
-        for block in (me, east, west):
-            greet(at(block, gy - 1))
-
-    @pl.when(is_top)
-    def _():
-        for _, block, own, _ in strips:
-            if own:
-
-                @pl.when(block != me)
-                def _(block=block):
-                    greet(at(block, gy))
-            else:
-                greet(at(block, gy))
-
     def load(src, dst, sem):
         copy = pltpu.make_async_copy(src, dst, sem)
         copy.start()
         return copy
 
-    load_u = load(ocean_u, F.at[LEV : 2 * LEV, 8 : 8 + ROWS, :], in_sem.at[0])
-    load_v = load(ocean_v, F.at[2 * LEV : 3 * LEV, 8 : 8 + ROWS, :], in_sem.at[1])
-    load_t = load(tracer, F.at[0:LEV, 8 : 8 + ROWS, :], in_sem.at[3])
+    def load_planes(src, g, sem):
+        for q in quarters:
+            load(src.at[q], F.at[g * LEV + q.start : g * LEV + q.stop, 8 : 8 + ROWS, :], sem)
+        return pltpu.make_async_copy(src, F.at[g * LEV : (g + 1) * LEV, 8 : 8 + ROWS, :], sem)
+
+    load_u = load_planes(ocean_u, 1, in_sem.at[0])
+    load_v = load_planes(ocean_v, 2, in_sem.at[1])
     small = [
         load(ocean_mask, OM, in_sem.at[2]),
         load(remap_in, remap, in_sem.at[4]),
@@ -168,6 +160,35 @@
         load(fold_in, fold_partner, in_sem.at[7]),
         load(remap_in, remap_wide, in_sem.at[8]),
     ]
+    barrier = pltpu.get_barrier_semaphore()
+
+    def greet(target):
+        pl.semaphore_signal(barrier, inc=1, device_id=target, device_id_type=MESH)
+
+    greet(at(east, gy))
+    greet(at(west, gy))
+
+    @pl.when(has_north)
+    def _():
+        for block in (me, east, west):
+            greet(at(block, gy + 1))
+
+    @pl.when(has_south)
+    def _():
+        for block in (me, east, west):
+            greet(at(block, gy - 1))
+
+    @pl.when(is_top)
+    def _():
+        for _, block, own, _ in strips:
+            if own:
+
+                @pl.when(block != me)
+                def _(block=block):
+                    greet(at(block, gy))
+            else:
+                greet(at(block, gy))
+
     ice_in = (ice_u, ice_v, ice_mass, ice_strength, ice_mask)
 
     def ice_place(i, half):
@@ -188,7 +209,8 @@
         X[:, south8, 0:COLS] = jnp.zeros((NF, 8, COLS), jnp.float32)
         EBS[...] = jnp.zeros((8, COLS), jnp.float32)
         WBS[...] = jnp.zeros((8, COLS), jnp.float32)
-        F[:, 0:8, :] = jnp.zeros((PLANES, 8, COLS), jnp.float32)
+        SR[...] = jnp.zeros((3 * LEV, COLS), jnp.float32)
+        SK[...] = jnp.zeros((8, COLS), jnp.float32)
 
     @pl.when(is_top)
     def _():
@@ -227,7 +249,9 @@
         copy.start()
         ice_away.append(copy)
 
+    load_t = load_planes(tracer, 0, in_sem.at[3])
     lane = lax.broadcasted_iota(jnp.int32, (1, COLS), 1)
+    even = (lane & 1) == 0
     row8 = lax.broadcasted_iota(jnp.int32, (8, 1), 0)
     tile_rows = slice(TOP, TOP + ROWS)
 
@@ -247,10 +271,41 @@
         X[5 + i, tile_rows, 0:COLS] = base
         F[SEA + 1 + i, 8 : 8 + ROWS, :] = spread
 
+    first = [(3 * t + p, SEA + p, slice(8 + 8 * t, 16 + 8 * t)) for t in range(ROWS // 8) for p in range(3)]
+    packed = jnp.zeros((8, COLS), jnp.float32)
+    for m, f, rows in first:
+        packed = jnp.where((lane >> 1) == m, pltpu.roll(F[f, rows, :], 2 * m + 1, 1), packed)
+    CK[...] = packed
+    for p in range(3):
+        TK[p : p + 1, :] = F[SEA + p, 87:88, :]
+        BK[p : p + 1, :] = F[SEA + p, 8:9, :]
+    first_e = send(CK, RKW, first_send.at[0], first_recv.at[0], at(east, gy))
+    first_w = send(CK, RKE, first_send.at[1], first_recv.at[1], at(west, gy))
+    first_n = send(TK, SK, first_send.at[2], first_recv.at[2], at(me, gy + 1))
+    first_s = send(BK, NK, first_send.at[3], first_recv.at[3], at(me, gy - 1))
+    first_f = send(TK, NK, first_send.at[4], first_recv.at[4], at(mirror, gy))
+    first_e.start()
+    first_w.start()
+
+    @pl.when(has_north)
+    def _():
+        first_n.start()
+
+    @pl.when(has_south)
+    def _():
+        first_s.start()
+
+    @pl.when(is_top)
+    def _():
+        first_f.start()
+
     load_t.wait()
-    row_n = send(F.at[:, 87:88, :], F.at[:, 7:8, :], edge_send.at[2], edge_recv.at[2], at(me, gy + 1))
-    row_s = send(F.at[:, 8:9, :], F.at[:, 88:89, :], edge_send.at[3], edge_recv.at[3], at(me, gy - 1))
-    row_f = send(F.at[:, 87:88, :], F.at[:, 88:89, :], edge_send.at[4], edge_recv.at[4], at(mirror, gy))
+    for f in range(3 * LEV):
+        TR[f : f + 1, :] = F[f, 87:88, :]
+        BR[f : f + 1, :] = F[f, 8:9, :]
+    row_n = send(TR, SR, edge_send.at[2], edge_recv.at[2], at(me, gy + 1))
+    row_s = send(BR, NR, edge_send.at[3], edge_recv.at[3], at(me, gy - 1))
+    row_f = send(TR, NR, edge_send.at[4], edge_recv.at[4], at(mirror, gy))
 
     @pl.when(has_north)
     def _():
@@ -267,8 +322,7 @@
     def pack(f, packed):
         return jnp.where((lane >> 1) == f, pltpu.roll(F[f, 8 : 8 + ROWS, :], 2 * f + 1, 1), packed)
 
-    packed = lax.fori_loop(0, PLANES, pack, jnp.zeros((ROWS, COLS), jnp.float32), unroll=3)
-    even = (lane & 1) == 0
+    packed = lax.fori_loop(0, 3 * LEV, pack, jnp.zeros((ROWS, COLS), jnp.float32), unroll=3)
     CE[...] = jnp.where(even, packed[0:HALF], pltpu.roll(packed[HALF:ROWS], 1, 1))
     CW[...] = jnp.where(even, pltpu.roll(packed[HALF:ROWS], COLS - 1, 1), packed[0:HALF])
     col_to_e = send(CE, RW, edge_send.at[0], edge_recv.at[0], at(east, gy))
@@ -290,54 +344,57 @@
         KK[rows, 256:512] = jnp.where(diagonal, low[k : k + 1], 0.0).astype(jnp.bfloat16)
         KK[rows, 512:768] = high_k
 
-    col_to_e.wait()
-    col_to_w.wait()
+    first_e.wait()
+    first_w.wait()
 
     @pl.when(has_north)
     def _():
-        row_n.wait_send()
-        row_s.wait_recv()
+        first_n.wait_send()
+        first_s.wait_recv()
 
     @pl.when(has_south)
     def _():
-        row_s.wait_send()
-        row_n.wait_recv()
-
+        first_s.wait_send()
+        first_n.wait_recv()
+
+    inside_here = fold_partner[...] - COLS * mirror
 
     @pl.when(is_top)
     def _():
-        row_f.wait()
-        inside = jnp.broadcast_to(fold_partner[...] - COLS * mirror, (8, COLS))
-
-        for f in range(SEA, PLANES):
-            taken = jnp.take_along_axis(F[f, 88:96, :], inside, axis=1, mode="promise_in_bounds")
-            F[f, 88:96, :] = taken if f == SEA else -taken
-
-    GE[0:HALF] = jnp.where(even, pltpu.roll(RE[...], COLS - 1, 1), pltpu.roll(RW[...], 1, 1))
-    GE[HALF:ROWS] = jnp.where(even, RE[...], RW[...])
-
-    def plane_sides(f):
+        first_f.wait()
+        inside = jnp.broadcast_to(inside_here, (8, COLS))
+        taken = jnp.take_along_axis(NK[...], inside, axis=1, mode="promise_in_bounds")
+        NK[...] = jnp.where(row8 == 0, taken, -taken)
+
+    GK[...] = jnp.where(even, pltpu.roll(RKE[...], COLS - 1, 1), pltpu.roll(RKW[...], 1, 1))
+    for p in range(3):
+        F[SEA + p, 88:89, :] = NK[p : p + 1, :]
+        F[SEA + p, 7:8, :] = SK[p : p + 1, :]
+
+    def sides_of(f, edges):
         value = F[f, 8 : 8 + ROWS, :]
-        edges = pltpu.roll(GE[...], COLS - 1 - 2 * f, 1)
         to_east = jnp.where(lane == COLS - 1, edges, pltpu.roll(value, COLS - 1, 1))
         to_west = jnp.where(lane == 0, edges, pltpu.roll(value, 1, 1))
         return value, to_east, to_west, F[f, 9 : 9 + ROWS, :], F[f, 7 : 7 + ROWS, :]
 
-    seas = plane_sides(SEA)
+    def first_edges(f):
+        return jnp.concatenate([pltpu.roll(GK[...], COLS - 1 - 2 * m, 1) for m, g, _ in first if g == f], axis=0)
+
+    def lap(f, edges):
+        value, to_east, to_west, to_north, to_south = sides_of(f, edges)
+        total = MK[0] * to_east + MK[1] * to_west + MK[2] * to_north + MK[3] * to_south
+        return value, total - MK[4] * value
+
+    seas = sides_of(SEA, first_edges(SEA))
     degree = jnp.zeros((ROWS, COLS), jnp.float32)
     for i in range(4):
         weight = seas[0] * seas[i + 1]
         MK[i] = weight
         degree = degree + weight
     MK[4] = degree
-
-    def lap(f):
-        value, to_east, to_west, to_north, to_south = plane_sides(f)
-        total = MK[0] * to_east + MK[1] * to_west + MK[2] * to_north + MK[3] * to_south
-        return value, total - MK[4] * value
-
     for i in range(2):
-        X[5 + i, tile_rows, 0:COLS] = X[5 + i, tile_rows, 0:COLS] + lap(SEA + 1 + i)[1]
+        f = SEA + 1 + i
+        X[5 + i, tile_rows, 0:COLS] = X[5 + i, tile_rows, 0:COLS] + lap(f, first_edges(f))[1]
 
     for i in range(5):
         ice_local[i].wait()
@@ -427,30 +484,45 @@
     @pl.when(is_top)
     def _():
         SS[0:NF] = X[0:NF, last8, 0:COLS]
-        inside = fold_partner[...] - COLS * mirror
-        SS[NF] = jnp.broadcast_to(inside.astype(jnp.float32), (8, COLS))
+        SS[NF] = jnp.broadcast_to(inside_here.astype(jnp.float32), (8, COLS))
         S[:, :, middle] = SS[...]
         strips_start(False)
 
+    col_to_e.wait()
+    col_to_w.wait()
+
+    @pl.when(has_north)
+    def _():
+        row_n.wait_send()
+        row_s.wait_recv()
+
+    @pl.when(has_south)
+    def _():
+        row_s.wait_send()
+        row_n.wait_recv()
+
+    @pl.when(is_top)
+    def _():
+        row_f.wait()
+        inside = jnp.broadcast_to(inside_here, (8, COLS))
+        for r in range(0, 3 * LEV, 8):
+            taken = jnp.take_along_axis(NR[r : r + 8, :], inside, axis=1, mode="promise_in_bounds")
+            NR[r : r + 8, :] = taken if r < LEV else -taken
+
+    for f in range(3 * LEV):
+        F[f, 88:89, :] = NR[f : f + 1, :]
+        F[f, 7:8, :] = SR[f : f + 1, :]
+    GE[0:HALF] = jnp.where(even, pltpu.roll(RE[...], COLS - 1, 1), pltpu.roll(RW[...], 1, 1))
+    GE[HALF:ROWS] = jnp.where(even, RE[...], RW[...])
+
     def diffuse(f, carry):
         coefficient = jnp.where(f < LEV, diffusivity[f & (LEV - 1)], viscosity[f & (LEV - 1)])
-        value, spread = lap(f)
+        value, spread = lap(f, pltpu.roll(GE[...], COLS - 1 - 2 * f, 1))
         new = value + coefficient * spread
         high = new.astype(jnp.bfloat16)
         DH[f] = high
         DL[f] = (new - high.astype(jnp.float32)).astype(jnp.bfloat16)
         return carry
-
-    @pl.when(is_top)
-    def _():
-        inside = jnp.broadcast_to(fold_partner[...] - COLS * mirror, (8, COLS))
-
-        def fold_edge(f, carry):
-            taken = jnp.take_along_axis(F[f, 88:96, :], inside, axis=1, mode="promise_in_bounds")
-            F[f, 88:96, :] = jnp.where(f < LEV, taken, -taken)
-            return carry
-
-        lax.fori_loop(0, 3 * LEV, fold_edge, 0, unroll=8)
 
     lax.fori_loop(0, 3 * LEV, diffuse, 0, unroll=4)
 
@@ -594,51 +666,22 @@
 
     low_piece, high_piece, low_tile, high_tile = slice(8, 16), slice(16, 24), slice(80, 88), slice(88, 96)
 
-    def top_cycles(cycles):
-        vel, sig, i_a, i_b = (S, SAB, 0, 1) if cycles[0] == 0 else (S2, S2, 2, 3)
-        for cycle in cycles:
-            left = 3 if cycle == cycles[0] else 1
-            close_top(XT, 0, vel, 0, -1)
-            close_top(XT, 1, vel, 1, -1)
+    def top_cycles():
+        for left in (3, 1):
+            close_top(XT, 0, S, 0, -1)
+            close_top(XT, 1, S, 1, -1)
             for win in windows(left):
                 cols = slice(COLS * win[0], COLS * win[1])
-                u, v = strip_sides(vel, 0, win, -1), strip_sides(vel, 1, win, -1)
-                old = (sig[i_a, :, cols], sig[i_b, :, cols]) if cycle else None
-                sig[i_a, :, cols], sig[i_b, :, cols] = stress(u, v, S[3, :, cols], old)
-            chunk_stress(XT, ABT, 8, cycle == 0)
-            close_top(ABT, 0, sig, i_a, 1)
-            close_top(ABT, 1, sig, i_b, 1)
+                u, v = strip_sides(S, 0, win, -1), strip_sides(S, 1, win, -1)
+                old = (SAB[0, :, cols], SAB[1, :, cols])
+                SAB[0, :, cols], SAB[1, :, cols] = stress(u, v, S[3, :, cols], old)
+            chunk_stress(XT, ABT, 8)
+            close_top(ABT, 0, SAB, 0, 1)
+            close_top(ABT, 1, SAB, 1, 1)
             for win in windows(left - 1):
                 cols = slice(COLS * win[0], COLS * win[1])
-                push(S, vel, every, cols, strip_sides(sig, i_a, win, 1), strip_sides(sig, i_b, win, 1))
+                push(S, S, every, cols, strip_sides(SAB, 0, win, 1), strip_sides(SAB, 1, win, 1))
             chunk_push(XT, ABT, 8)
-
-    for start in chunks:
-        ready(X, slice(start, start + CHUNK), slice(0, 2 * COLS))
-
-    @pl.when(is_top)
-    def _():
-        XT[...] = X[:, 72:112, :]
-        ABT[...] = jnp.zeros((2, 40, 2 * COLS), jnp.float32)
-
-    lax.fori_loop(0, 2, tile_cycle, 0)
-
-    @pl.when(is_top)
-    def _():
-        strips_arrive(False)
-        IDX[...] = jnp.broadcast_to(S[NF, 7:8, :], IDX.shape).astype(jnp.int32)
-        ready(S, every, slice(0, BLOCKS * COLS))
-        top_cycles((0, 1))
-        SS2[0:2] = XT[0:2, high_piece, 0:COLS]
-        SS2[2:4] = ABT[:, high_piece, 0:COLS]
-        strips_start(True)
-        S2[:, :, middle] = SS2[...]
-        X[0:2, high_tile, :] = XT[0:2, high_piece, :]
-        AB[:, high_tile, :] = ABT[:, high_piece, :]
-        XT[0:2, low_piece, :] = X[0:2, low_tile, :]
-        ABT[:, low_piece, :] = AB[:, low_tile, :]
-
-    lax.fori_loop(0, 2, tile_cycle, 0)
 
     away = pl.ds(pl.multiple_of(TOP + HALF * (1 - comp), 8), HALF)
     here = pl.ds(pl.multiple_of(TOP + HALF * comp, 8), HALF)
@@ -650,10 +693,58 @@
         pltpu.make_async_copy(X.at[i, here, 0:COLS], ice_out[i].at[:, mine], out_sem.at[3 + i]) for i in range(2)
     ]
 
-    @pl.when(jnp.logical_not(is_top))
-    def _():
-        for copy in vel_away + vel_here:
-            copy.start()
+    for start in chunks:
+        ready(X, slice(start, start + CHUNK), slice(0, 2 * COLS))
+
+    @pl.when(is_top)
+    def _():
+        XT[...] = X[:, 72:112, :]
+        ABT[...] = jnp.zeros((2, 40, 2 * COLS), jnp.float32)
+        SAB[...] = jnp.zeros((2, 8, BLOCKS * COLS), jnp.float32)
+
+    def two_cycles(phase, carry):
+        lax.fori_loop(0, 2, tile_cycle, 0)
+
+        @pl.when(is_top & (phase == 0))
+        def _():
+            strips_arrive(False)
+            IDX[...] = jnp.broadcast_to(S[NF, 7:8, :], IDX.shape).astype(jnp.int32)
+            ready(S, every, slice(0, BLOCKS * COLS))
+
+        @pl.when(is_top & (phase == 1))
+        def _():
+            strips_arrive(True)
+            to_the_e = S2[0:2, 7:8, COLS * (REACH + 1) : COLS * (REACH + 2)]
+            to_the_w = S2[0:2, 7:8, COLS * (REACH - 1) : COLS * REACH]
+            XT[0:2, 23:24, COLS : 2 * COLS] = jnp.where(lane < COLS // 2, to_the_e, to_the_w)
+            S[0:2] = S2[0:2]
+            SAB[...] = S2[2:4]
+
+        @pl.when(is_top)
+        def _():
+            top_cycles()
+
+        @pl.when(is_top & (phase == 0))
+        def _():
+            SS2[0:2] = XT[0:2, high_piece, 0:COLS]
+            SS2[2:4] = ABT[:, high_piece, 0:COLS]
+            strips_start(True)
+            S2[:, :, middle] = SS2[...]
+            X[0:2, high_tile, :] = XT[0:2, high_piece, :]
+            AB[:, high_tile, :] = ABT[:, high_piece, :]
+            XT[0:2, low_piece, :] = X[0:2, low_tile, :]
+            ABT[:, low_piece, :] = AB[:, low_tile, :]
+
+        return carry
+
+    lax.fori_loop(0, 2, two_cycles, 0)
+
+    @pl.when(is_top)
+    def _():
+        X[0:2, high_tile, :] = XT[0:2, high_piece, :]
+
+    for copy in vel_away + vel_here:
+        copy.start()
 
     def regrid(g):
         planes = pl.ds(g * LEV, LEV)
@@ -664,22 +755,6 @@
         for i, r in enumerate(pieces):
             O[planes, r : r + LEV, :] = new[:, COLS * i : COLS * (i + 1)].reshape(LEV, LEV, COLS)
 
-    @pl.when(is_top)
-    def _():
-        def early(g, carry):
-            regrid(g)
-            return carry
-
-        lax.fori_loop(0, 2, early, 0)
-        strips_arrive(True)
-        to_the_e = S2[0:2, 7:8, COLS * (REACH + 1) : COLS * (REACH + 2)]
-        to_the_w = S2[0:2, 7:8, COLS * (REACH - 1) : COLS * REACH]
-        XT[0:2, 23:24, COLS : 2 * COLS] = jnp.where(lane < COLS // 2, to_the_e, to_the_w)
-        top_cycles((2, 3))
-        X[0:2, high_tile, :] = XT[0:2, high_piece, :]
-        for copy in vel_away + vel_here:
-            copy.start()
-
     outs = (new_tracer, new_ocean_u, new_ocean_v)
 
     stores = [
@@ -687,10 +762,7 @@
     ]
 
     def finish(g, carry):
-        @pl.when(jnp.logical_not(is_top) | (g == 2))
-        def _():
-            regrid(g)
-
+        regrid(g)
         for i in range(3):
 
             @pl.when(g == i)
@@ -698,7 +770,10 @@
                 if i:
                     tau = X[i - 1, tile_rows, 0:COLS] - X[4 + i, tile_rows, 0:COLS] * (1.0 / SHARE)
                     O[i * LEV] = O[i * LEV] + COUPLE * (F[SEA, 8 : 8 + ROWS, :] * tau)
-                stores[i].start()
+                for q in quarters:
+                    pltpu.make_async_copy(
+                        O.at[i * LEV + q.start : i * LEV + q.stop], outs[i].at[q], out_sem.at[i]
+                    ).start()
 
         return carry
 
@@ -721,7 +796,10 @@
     count = len(refs) // 2
     sems = refs[-1]
     copies = [pltpu.make_async_copy(refs[i], refs[count + i], sems.at[i]) for i in range(count)]
-    for copy in copies:
+    for i in range(3):
+        for q in quarters:
+            pltpu.make_async_copy(refs[i].at[q], refs[count + i].at[q], sems.at[i]).start()
+    for copy in copies[3:]:
         copy.start()
     for copy in copies:
         copy.wait()
@@ -777,6 +855,11 @@
                 vmem((8, COLS), f32),
                 vmem((8, COLS), f32),
                 vmem((8, COLS), f32),
+                vmem((3 * LEV, COLS), f32),
+                vmem((3 * LEV, COLS), f32),
+                vmem((3 * LEV, COLS), f32),
+                vmem((3 * LEV, COLS), f32),
+                *[vmem((8, COLS), f32)] * 8,
                 vmem((HALF, COLS), f32),
                 vmem((HALF, COLS), f32),
                 vmem((HALF, COLS), f32),
@@ -792,6 +875,8 @@
                 vmem((LEV, LEV), f32),
                 vmem((1, COLS), jnp.int32),
                 dma((9,)),
+                dma((5,)),
+                dma((5,)),
                 dma((5,)),
                 dma((5,)),
                 dma((5,)),

time: 28.6 us -> 29.6 us (1.035)
  Pallas kernels: 27.8 us -> 28.9 us
    pallas_call x1, Pallas kernels: 26.5 us -> 27.6 us  [body(): pl.pallas_call(step, out_shape=shapes, in_specs=[main_memory] * 13, out_s...]
where the time goes in v3:
time: 29.6 us; the launch traced here: 29.5 us
  Pallas kernels  28.9 us (98%)
  between operations  0.64 us (2%)
    pallas_call x1, Pallas kernels, body(): pl.pallas_call(step, out_shape=shapes, in_specs=[main_memory] * 13, out_s...  27.6 us
    pallas_call x1, Pallas kernels, body(): pl.pallas_call(deliver, out_shape=shapes, in_specs=[anywhere] * 5, out_sp...  1.32 us

profile of v3, /device:TPU:224, one launch (start us, length us, event | category | flops | bytes accessed | tf_op | source)
XLA Modules:
  0.0 29.5 jit_solution(10264491895586102408)
XLA Ops:
  0.6 27.6 %shard_map.164 = (f32[16,80,128]{2,1,0:T(8,128)S(1)}, f32[16,80,128]{2,1,0:T(8,128)S(1)}, f32[16,80,128]{2,1,0:T(8,128)S(1)}, f32[40,256]{1,0:T(8,128)S(1)}, f32[40,256]{1,0:T(8,128)S(1)}) custom-call(f32[16,80,128]{2,1,0:T(8,128)} %args_0_.4, f32[16,80,128]{2,1,0:T(8,128)} %args_1_.4, f32[16,80,128]{2,1,0:T(8,128)} %args_2_.4, s32[80,128]{1,0:T(8,128)} %args_3_.4, ...), custom_call_target="tpu_custom_call" | custom-call | tf_op jit(solution)/shard_map/pallas_call | solution.py:830
  28.2 1.3 %shard_map.165 = (f32[16,80,128]{2,1,0:T(8,128)}, f32[16,80,128]{2,1,0:T(8,128)}, f32[16,80,128]{2,1,0:T(8,128)}, f32[40,256]{1,0:T(8,128)}, f32[40,256]{1,0:T(8,128)}) custom-call(f32[16,80,128]{2,1,0:T(8,128)S(1)} %get-tuple-element.10.refs_0_, f32[16,80,128]{2,1,0:T(8,128)S(1)} %get-tuple-element.11.refs_1_, ...), custom_call_target="tpu_custom_call" | custom-call | tf_op jit(solution)/shard_map/pallas_call | solution.py:914

commit v4 on v3

--- a/solution.py
+++ b/solution.py
@@ -28,9 +28,6 @@
 MIRROR_ROWS = (4, 3, 2)
 SEA = 3 * LEV
 PLANES = SEA + 3
-
-
-quarters = [slice(4 * i, 4 * i + 4) for i in range(LEV // 4)]
 
 
 def kernel(
@@ -52,8 +49,7 @@
     new_tracer,
     new_ocean_u,
     new_ocean_v,
-    new_ice_u,
-    new_ice_v,
+    new_ice,
     F,
     DH,
     DL,
@@ -145,13 +141,37 @@
         copy.start()
         return copy
 
-    def load_planes(src, g, sem):
-        for q in quarters:
-            load(src.at[q], F.at[g * LEV + q.start : g * LEV + q.stop, 8 : 8 + ROWS, :], sem)
-        return pltpu.make_async_copy(src, F.at[g * LEV : (g + 1) * LEV, 8 : 8 + ROWS, :], sem)
-
-    load_u = load_planes(ocean_u, 1, in_sem.at[0])
-    load_v = load_planes(ocean_v, 2, in_sem.at[1])
+    load_u = load(ocean_u, F.at[LEV : 2 * LEV, 8 : 8 + ROWS, :], in_sem.at[0])
+    load_v = load(ocean_v, F.at[2 * LEV : 3 * LEV, 8 : 8 + ROWS, :], in_sem.at[1])
+    barrier = pltpu.get_barrier_semaphore()
+
+    def greet(target):
+        pl.semaphore_signal(barrier, inc=1, device_id=target, device_id_type=MESH)
+
+    greet(at(east, gy))
+    greet(at(west, gy))
+
+    @pl.when(has_north)
+    def _():
+        for block in (me, east, west):
+            greet(at(block, gy + 1))
+
+    @pl.when(has_south)
+    def _():
+        for block in (me, east, west):
+            greet(at(block, gy - 1))
+
+    @pl.when(is_top)
+    def _():
+        for _, block, own, _ in strips:
+            if own:
+
+                @pl.when(block != me)
+                def _(block=block):
+                    greet(at(block, gy))
+            else:
+                greet(at(block, gy))
+
     small = [
         load(ocean_mask, OM, in_sem.at[2]),
         load(remap_in, remap, in_sem.at[4]),
@@ -160,35 +180,6 @@
         load(fold_in, fold_partner, in_sem.at[7]),
         load(remap_in, remap_wide, in_sem.at[8]),
     ]
-    barrier = pltpu.get_barrier_semaphore()
-
-    def greet(target):
-        pl.semaphore_signal(barrier, inc=1, device_id=target, device_id_type=MESH)
-
-    greet(at(east, gy))
-    greet(at(west, gy))
-
-    @pl.when(has_north)
-    def _():
-        for block in (me, east, west):
-            greet(at(block, gy + 1))
-
-    @pl.when(has_south)
-    def _():
-        for block in (me, east, west):
-            greet(at(block, gy - 1))
-
-    @pl.when(is_top)
-    def _():
-        for _, block, own, _ in strips:
-            if own:
-
-                @pl.when(block != me)
-                def _(block=block):
-                    greet(at(block, gy))
-            else:
-                greet(at(block, gy))
-
     ice_in = (ice_u, ice_v, ice_mass, ice_strength, ice_mask)
 
     def ice_place(i, half):
@@ -199,7 +190,8 @@
 
     mine = pl.ds(pl.multiple_of(COLS * comp, COLS), COLS)
     other = pl.ds(pl.multiple_of(COLS * (1 - comp), COLS), COLS)
-    ice_local = [load(ice_in[i].at[:, mine], ice_place(i, comp), ice_sem.at[i]) for i in range(5)]
+    for i in range(5):
+        load(ice_in[i].at[:, mine], ice_place(i, comp), ice_sem.at[0])
 
     first8, last8 = slice(TOP, TOP + 8), slice(TOP + ROWS - 8, TOP + ROWS)
     south8, north8 = slice(TOP - 8, TOP), slice(TOP + ROWS, TOP + ROWS + 8)
@@ -241,15 +233,12 @@
         )
         return copy
 
-    ice_away = []
     for i in range(5):
-        copy = send(
-            ice_in[i].at[:, other], ice_place(i, comp), ice_send.at[i], ice_recv.at[i], partner
-        )
-        copy.start()
-        ice_away.append(copy)
-
-    load_t = load_planes(tracer, 0, in_sem.at[3])
+        send(ice_in[i].at[:, other], ice_place(i, comp), ice_send.at[0], ice_recv.at[0], partner).start()
+    ice_all = X.at[0:5, TOP : TOP + HALF, 0:COLS]
+    ice_away = send(ice_all, ice_all, ice_send.at[0], ice_recv.at[0], partner)
+
+    load_t = load(tracer, F.at[0:LEV, 8 : 8 + ROWS, :], in_sem.at[3])
     lane = lax.broadcasted_iota(jnp.int32, (1, COLS), 1)
     even = (lane & 1) == 0
     row8 = lax.broadcasted_iota(jnp.int32, (8, 1), 0)
@@ -396,9 +385,8 @@
         f = SEA + 1 + i
         X[5 + i, tile_rows, 0:COLS] = X[5 + i, tile_rows, 0:COLS] + lap(f, first_edges(f))[1]
 
-    for i in range(5):
-        ice_local[i].wait()
-        ice_away[i].wait_recv()
+    pltpu.make_async_copy(ice_all, ice_all, ice_sem.at[0]).wait()
+    ice_away.wait_recv()
     X[4, tile_rows, 0:COLS] = IM[...].astype(jnp.float32)
 
 
@@ -432,10 +420,10 @@
         kept = slice(8 - rows, 8)
         return src.at[:, kept, :], dst.at[:, kept, COLS * slot : COLS * (slot + 1)]
 
-    def strip_copy(again, slot, block, rows):
+    def strip_copy(again, slot, block, own, rows):
         src, dst = strip_ends(SS2, S2, slot, rows) if again else strip_ends(SS, S, slot, rows)
         sent, received = (again_send, again_recv) if again else (strip_send, strip_recv)
-        return send(src, dst, sent.at[slot], received.at[slot], at(block, gy))
+        return send(src, dst, sent.at[slot if own else 0], received.at[0], at(block, gy))
 
     def strips_start(again):
         for slot, block, own, rows in strips:
@@ -443,28 +431,31 @@
 
                 @pl.when(block != me)
                 def _(slot=slot, block=block, rows=rows):
-                    strip_copy(again, slot, block, rows).start()
+                    strip_copy(again, slot, block, True, rows).start()
 
                 @pl.when(block == me)
                 def _(slot=slot, rows=rows):
                     src, dst = strip_ends(SS2, S2, slot, rows) if again else strip_ends(SS, S, slot, rows)
-                    pltpu.make_async_copy(src, dst, (again_recv if again else strip_recv).at[slot]).start()
+                    pltpu.make_async_copy(src, dst, (again_recv if again else strip_recv).at[0]).start()
             else:
-                strip_copy(again, slot, block, rows).start()
+                strip_copy(again, slot, block, False, rows).start()
+
+    def strips_all(again, rows):
+        area = (S2 if again else S).at[:, 0:1, 0 : COLS * rows]
+        sent, received = (again_send, again_recv) if again else (strip_send, strip_recv)
+        return send(area, area, sent.at[0], received.at[0], partner)
 
     def strips_arrive(again):
-        for slot, block, own, rows in strips:
-            strip_copy(again, slot, block, rows).wait_recv()
+        strips_all(again, sum(rows for _, _, _, rows in strips)).wait_recv()
 
     def strips_sent(again):
+        strips_all(again, sum(rows for _, _, own, rows in strips if not own)).wait_send()
         for slot, block, own, rows in strips:
             if own:
 
                 @pl.when(block != me)
                 def _(slot=slot, block=block, rows=rows):
-                    strip_copy(again, slot, block, rows).wait_send()
-            else:
-                strip_copy(again, slot, block, rows).wait_send()
+                    strip_copy(again, slot, block, True, rows).wait_send()
 
     middle = slice(COLS * REACH, COLS * (REACH + 1))
 
@@ -666,85 +657,61 @@
 
     low_piece, high_piece, low_tile, high_tile = slice(8, 16), slice(16, 24), slice(80, 88), slice(88, 96)
 
-    def top_cycles():
-        for left in (3, 1):
-            close_top(XT, 0, S, 0, -1)
-            close_top(XT, 1, S, 1, -1)
+    def top_cycles(cycles):
+        vel, sig, i_a, i_b = (S, SAB, 0, 1) if cycles[0] == 0 else (S2, S2, 2, 3)
+        for cycle in cycles:
+            left = 3 if cycle == cycles[0] else 1
+            close_top(XT, 0, vel, 0, -1)
+            close_top(XT, 1, vel, 1, -1)
             for win in windows(left):
                 cols = slice(COLS * win[0], COLS * win[1])
-                u, v = strip_sides(S, 0, win, -1), strip_sides(S, 1, win, -1)
-                old = (SAB[0, :, cols], SAB[1, :, cols])
-                SAB[0, :, cols], SAB[1, :, cols] = stress(u, v, S[3, :, cols], old)
-            chunk_stress(XT, ABT, 8)
-            close_top(ABT, 0, SAB, 0, 1)
-            close_top(ABT, 1, SAB, 1, 1)
+                u, v = strip_sides(vel, 0, win, -1), strip_sides(vel, 1, win, -1)
+                old = (sig[i_a, :, cols], sig[i_b, :, cols]) if cycle else None
+                sig[i_a, :, cols], sig[i_b, :, cols] = stress(u, v, S[3, :, cols], old)
+            chunk_stress(XT, ABT, 8, cycle == 0)
+            close_top(ABT, 0, sig, i_a, 1)
+            close_top(ABT, 1, sig, i_b, 1)
             for win in windows(left - 1):
                 cols = slice(COLS * win[0], COLS * win[1])
-                push(S, S, every, cols, strip_sides(SAB, 0, win, 1), strip_sides(SAB, 1, win, 1))
+                push(S, vel, every, cols, strip_sides(sig, i_a, win, 1), strip_sides(sig, i_b, win, 1))
             chunk_push(XT, ABT, 8)
+
+    for start in chunks:
+        ready(X, slice(start, start + CHUNK), slice(0, 2 * COLS))
+
+    @pl.when(is_top)
+    def _():
+        XT[...] = X[:, 72:112, :]
+        ABT[...] = jnp.zeros((2, 40, 2 * COLS), jnp.float32)
+
+    lax.fori_loop(0, 2, tile_cycle, 0)
+
+    @pl.when(is_top)
+    def _():
+        strips_arrive(False)
+        IDX[...] = jnp.broadcast_to(S[NF, 7:8, 0 : BLOCKS * COLS], IDX.shape).astype(jnp.int32)
+        ready(S, every, slice(0, BLOCKS * COLS))
+        top_cycles((0, 1))
+        SS2[0:2] = XT[0:2, high_piece, 0:COLS]
+        SS2[2:4] = ABT[:, high_piece, 0:COLS]
+        strips_start(True)
+        S2[:, :, middle] = SS2[...]
+        X[0:2, high_tile, :] = XT[0:2, high_piece, :]
+        AB[:, high_tile, :] = ABT[:, high_piece, :]
+        XT[0:2, low_piece, :] = X[0:2, low_tile, :]
+        ABT[:, low_piece, :] = AB[:, low_tile, :]
+
+    lax.fori_loop(0, 2, tile_cycle, 0)
 
     away = pl.ds(pl.multiple_of(TOP + HALF * (1 - comp), 8), HALF)
     here = pl.ds(pl.multiple_of(TOP + HALF * comp, 8), HALF)
-    ice_out = (new_ice_u, new_ice_v)
-    vel_away = [
-        send(X.at[i, away, 0:COLS], ice_out[i].at[:, mine], vel_send.at[i], vel_recv.at[i], partner) for i in range(2)
-    ]
-    vel_here = [
-        pltpu.make_async_copy(X.at[i, here, 0:COLS], ice_out[i].at[:, mine], out_sem.at[3 + i]) for i in range(2)
-    ]
-
-    for start in chunks:
-        ready(X, slice(start, start + CHUNK), slice(0, 2 * COLS))
-
-    @pl.when(is_top)
-    def _():
-        XT[...] = X[:, 72:112, :]
-        ABT[...] = jnp.zeros((2, 40, 2 * COLS), jnp.float32)
-        SAB[...] = jnp.zeros((2, 8, BLOCKS * COLS), jnp.float32)
-
-    def two_cycles(phase, carry):
-        lax.fori_loop(0, 2, tile_cycle, 0)
-
-        @pl.when(is_top & (phase == 0))
-        def _():
-            strips_arrive(False)
-            IDX[...] = jnp.broadcast_to(S[NF, 7:8, :], IDX.shape).astype(jnp.int32)
-            ready(S, every, slice(0, BLOCKS * COLS))
-
-        @pl.when(is_top & (phase == 1))
-        def _():
-            strips_arrive(True)
-            to_the_e = S2[0:2, 7:8, COLS * (REACH + 1) : COLS * (REACH + 2)]
-            to_the_w = S2[0:2, 7:8, COLS * (REACH - 1) : COLS * REACH]
-            XT[0:2, 23:24, COLS : 2 * COLS] = jnp.where(lane < COLS // 2, to_the_e, to_the_w)
-            S[0:2] = S2[0:2]
-            SAB[...] = S2[2:4]
-
-        @pl.when(is_top)
-        def _():
-            top_cycles()
-
-        @pl.when(is_top & (phase == 0))
-        def _():
-            SS2[0:2] = XT[0:2, high_piece, 0:COLS]
-            SS2[2:4] = ABT[:, high_piece, 0:COLS]
-            strips_start(True)
-            S2[:, :, middle] = SS2[...]
-            X[0:2, high_tile, :] = XT[0:2, high_piece, :]
-            AB[:, high_tile, :] = ABT[:, high_piece, :]
-            XT[0:2, low_piece, :] = X[0:2, low_tile, :]
-            ABT[:, low_piece, :] = AB[:, low_tile, :]
-
-        return carry
-
-    lax.fori_loop(0, 2, two_cycles, 0)
-
-    @pl.when(is_top)
-    def _():
-        X[0:2, high_tile, :] = XT[0:2, high_piece, :]
-
-    for copy in vel_away + vel_here:
-        copy.start()
+    vel_away = send(X.at[0:2, away, 0:COLS], new_ice.at[:, :, mine], vel_send.at[0], vel_recv.at[0], partner)
+    vel_here = pltpu.make_async_copy(X.at[0:2, here, 0:COLS], new_ice.at[:, :, mine], out_sem.at[3])
+
+    @pl.when(jnp.logical_not(is_top))
+    def _():
+        vel_away.start()
+        vel_here.start()
 
     def regrid(g):
         planes = pl.ds(g * LEV, LEV)
@@ -755,6 +722,22 @@
         for i, r in enumerate(pieces):
             O[planes, r : r + LEV, :] = new[:, COLS * i : COLS * (i + 1)].reshape(LEV, LEV, COLS)
 
+    @pl.when(is_top)
+    def _():
+        def early(g, carry):
+            regrid(g)
+            return carry
+
+        lax.fori_loop(0, 2, early, 0)
+        strips_arrive(True)
+        to_the_e = S2[0:2, 7:8, COLS * (REACH + 1) : COLS * (REACH + 2)]
+        to_the_w = S2[0:2, 7:8, COLS * (REACH - 1) : COLS * REACH]
+        XT[0:2, 23:24, COLS : 2 * COLS] = jnp.where(lane < COLS // 2, to_the_e, to_the_w)
+        top_cycles((2, 3))
+        X[0:2, high_tile, :] = XT[0:2, high_piece, :]
+        vel_away.start()
+        vel_here.start()
+
     outs = (new_tracer, new_ocean_u, new_ocean_v)
 
     stores = [
@@ -762,7 +745,10 @@
     ]
 
     def finish(g, carry):
-        regrid(g)
+        @pl.when(jnp.logical_not(is_top) | (g == 2))
+        def _():
+            regrid(g)
+
         for i in range(3):
 
             @pl.when(g == i)
@@ -770,10 +756,7 @@
                 if i:
                     tau = X[i - 1, tile_rows, 0:COLS] - X[4 + i, tile_rows, 0:COLS] * (1.0 / SHARE)
                     O[i * LEV] = O[i * LEV] + COUPLE * (F[SEA, 8 : 8 + ROWS, :] * tau)
-                for q in quarters:
-                    pltpu.make_async_copy(
-                        O.at[i * LEV + q.start : i * LEV + q.stop], outs[i].at[q], out_sem.at[i]
-                    ).start()
+                stores[i].start()
 
         return carry
 
@@ -784,22 +767,22 @@
         strips_sent(False)
         strips_sent(True)
 
-    for copy in ice_away:
-        copy.wait_send()
-    for copy in vel_away:
+    ice_away.wait_send()
+    vel_away.wait()
+    for copy in [vel_here] + stores:
         copy.wait()
-    for copy in vel_here + stores:
-        copy.wait()
-
-
-def deliver(*refs):
-    count = len(refs) // 2
-    sems = refs[-1]
-    copies = [pltpu.make_async_copy(refs[i], refs[count + i], sems.at[i]) for i in range(count)]
-    for i in range(3):
-        for q in quarters:
-            pltpu.make_async_copy(refs[i].at[q], refs[count + i].at[q], sems.at[i]).start()
-    for copy in copies[3:]:
+
+
+def deliver(tracer, ocean_u, ocean_v, ice, new_tracer, new_ocean_u, new_ocean_v, new_ice_u, new_ice_v, sems):
+    pairs = [
+        (tracer, new_tracer),
+        (ocean_u, new_ocean_u),
+        (ocean_v, new_ocean_v),
+        (ice.at[0], new_ice_u),
+        (ice.at[1], new_ice_v),
+    ]
+    copies = [pltpu.make_async_copy(src, dst, sems.at[i]) for i, (src, dst) in enumerate(pairs)]
+    for copy in copies:
         copy.start()
     for copy in copies:
         copy.wait()
@@ -829,9 +812,9 @@
         shapes = (ocean_shape, ocean_shape, ocean_shape, ice_shape, ice_shape)
         results = pl.pallas_call(
             step,
-            out_shape=shapes,
+            out_shape=(*shapes[:3], jax.ShapeDtypeStruct((2, *ice_fields[0].shape), f32)),
             in_specs=[main_memory] * 13,
-            out_specs=(anywhere,) * 5,
+            out_specs=(anywhere,) * 4,
             scratch_shapes=[
                 vmem((PLANES, 96, COLS), f32),
                 vmem((3 * LEV, ROWS, COLS), jnp.bfloat16),
@@ -842,10 +825,10 @@
                 vmem((2, 112, 2 * COLS), f32),
                 vmem((NF, 40, 2 * COLS), f32),
                 vmem((2, 40, 2 * COLS), f32),
-                vmem((NS, 8, BLOCKS * COLS), f32),
+                vmem((NS, 8, 2 * BLOCKS * COLS), f32),
                 vmem((2, 8, BLOCKS * COLS), f32),
                 vmem((NS, 8, COLS), f32),
-                vmem((4, 8, BLOCKS * COLS), f32),
+                vmem((4, 8, 2 * BLOCKS * COLS), f32),
                 vmem((4, 8, COLS), f32),
                 vmem((HALF, COLS), f32),
                 vmem((HALF, COLS), f32),
@@ -914,7 +897,7 @@
         return pl.pallas_call(
             deliver,
             out_shape=shapes,
-            in_specs=[anywhere] * 5,
+            in_specs=[anywhere] * 4,
             out_specs=(main_memory,) * 5,
             scratch_shapes=[dma((5,))],
             compiler_params=pltpu.CompilerParams(vmem_limit_bytes=1024 * 1024),

time: 29.6 us -> 27.8 us (0.939)
  Pallas kernels: 28.9 us -> 27 us
    pallas_call x2, Pallas kernels: 28.9 us -> 27 us  [the longest x1 25.7 us: body(): pl.pallas_call(step, out_shape=(*shapes[:3], jax.ShapeDtypeStruct((2, *ic...]
where the time goes in v4:
time: 27.8 us; the launch traced here: 27.7 us
  Pallas kernels  27 us (97%)
  between operations  0.64 us (2%)
    pallas_call x1, Pallas kernels, body(): pl.pallas_call(step, out_shape=(*shapes[:3], jax.ShapeDtypeStruct((2, *ic...  25.7 us
    pallas_call x1, Pallas kernels, body(): pl.pallas_call(deliver, out_shape=shapes, in_specs=[anywhere] * 4, out_sp...  1.32 us

profile of v4, /device:TPU:224, one launch (start us, length us, event | category | flops | bytes accessed | tf_op | source)
XLA Modules:
  0.0 27.7 jit_solution(3797257382018920459)
XLA Ops:
  0.6 25.7 %shard_map.164 = (f32[16,80,128]{2,1,0:T(8,128)S(1)}, f32[16,80,128]{2,1,0:T(8,128)S(1)}, f32[16,80,128]{2,1,0:T(8,128)S(1)}, f32[2,40,256]{2,1,0:T(8,128)S(1)}) custom-call(f32[16,80,128]{2,1,0:T(8,128)} %args_0_.4, f32[16,80,128]{2,1,0:T(8,128)} %args_1_.4, f32[16,80,128]{2,1,0:T(8,128)} %args_2_.4, s32[80,128]{1,0:T(8,128)} %args_3_.4, f32[16]{0:T(128)} %args_4_.4, ...), custom_call_target="tpu_custom_call" | custom-call | tf_op jit(solution)/shard_map/pallas_call | solution.py:813
  26.4 1.3 %shard_map.165 = (f32[16,80,128]{2,1,0:T(8,128)}, f32[16,80,128]{2,1,0:T(8,128)}, f32[16,80,128]{2,1,0:T(8,128)}, f32[40,256]{1,0:T(8,128)}, f32[40,256]{1,0:T(8,128)}) custom-call(f32[16,80,128]{2,1,0:T(8,128)S(1)} %get-tuple-element.9.tracer, f32[16,80,128]{2,1,0:T(8,128)S(1)} %get-tuple-element.10.ocean_u, f32[16,80,128]{2,1,0:T(8,128)S(1)} %get-tuple-element.11.ocean_v, ...), custom_call_target="tpu_custom_call" | custom-call | tf_op jit(solution)/shard_map/pallas_call | solution.py:897

commit v5 on v4

--- a/solution.py
+++ b/solution.py
@@ -515,7 +515,7 @@
         DL[f] = (new - high.astype(jnp.float32)).astype(jnp.bfloat16)
         return carry
 
-    lax.fori_loop(0, 3 * LEV, diffuse, 0, unroll=4)
+    lax.fori_loop(0, 2 * LEV, diffuse, 0, unroll=4)
 
     to_e.wait()
     to_w.wait()
@@ -703,14 +703,22 @@
 
     lax.fori_loop(0, 2, tile_cycle, 0)
 
-    away = pl.ds(pl.multiple_of(TOP + HALF * (1 - comp), 8), HALF)
     here = pl.ds(pl.multiple_of(TOP + HALF * comp, 8), HALF)
-    vel_away = send(X.at[0:2, away, 0:COLS], new_ice.at[:, :, mine], vel_send.at[0], vel_recv.at[0], partner)
+
+    def vel_part(i, low, rows):
+        away = pl.ds(pl.multiple_of(TOP + HALF * (1 - comp) + low, 8), rows)
+        return send(
+            X.at[0:2, away, 0:COLS], new_ice.at[:, low : low + rows, mine], vel_send.at[i], vel_recv.at[i], partner
+        )
+
+    vel_away = [vel_part(0, 0, HALF - 8), vel_part(1, HALF - 8, 8)]
     vel_here = pltpu.make_async_copy(X.at[0:2, here, 0:COLS], new_ice.at[:, :, mine], out_sem.at[3])
 
+    vel_away[0].start()
+
     @pl.when(jnp.logical_not(is_top))
     def _():
-        vel_away.start()
+        vel_away[1].start()
         vel_here.start()
 
     def regrid(g):
@@ -735,8 +743,10 @@
         XT[0:2, 23:24, COLS : 2 * COLS] = jnp.where(lane < COLS // 2, to_the_e, to_the_w)
         top_cycles((2, 3))
         X[0:2, high_tile, :] = XT[0:2, high_piece, :]
-        vel_away.start()
+        vel_away[1].start()
         vel_here.start()
+
+    lax.fori_loop(2 * LEV, 3 * LEV, diffuse, 0, unroll=4)
 
     outs = (new_tracer, new_ocean_u, new_ocean_v)
 
@@ -768,8 +778,7 @@
         strips_sent(True)
 
     ice_away.wait_send()
-    vel_away.wait()
-    for copy in [vel_here] + stores:
+    for copy in vel_away + [vel_here] + stores:
         copy.wait()
 
 

time: 27.8 us -> 27.5 us (0.989)
  Pallas kernels: 27 us -> 26.7 us
    pallas_call x1, Pallas kernels: 25.7 us -> 25.4 us  [body(): pl.pallas_call(step, out_shape=(*shapes[:3], jax.ShapeDtypeStruct((2, *ic...]
where the time goes in v5:
time: 27.5 us; the launch traced here: 27.4 us
  Pallas kernels  26.7 us (97%)
  between operations  0.64 us (2%)
    pallas_call x1, Pallas kernels, body(): pl.pallas_call(step, out_shape=(*shapes[:3], jax.ShapeDtypeStruct((2, *ic...  25.4 us
    pallas_call x1, Pallas kernels, body(): pl.pallas_call(deliver, out_shape=shapes, in_specs=[anywhere] * 4, out_sp...  1.32 us

profile of v5, /device:TPU:224, one launch (start us, length us, event | category | flops | bytes accessed | tf_op | source)
XLA Modules:
  0.0 27.4 jit_solution(8141413160319272453)
XLA Ops:
  0.6 25.4 %shard_map.164 = (f32[16,80,128]{2,1,0:T(8,128)S(1)}, f32[16,80,128]{2,1,0:T(8,128)S(1)}, f32[16,80,128]{2,1,0:T(8,128)S(1)}, f32[2,40,256]{2,1,0:T(8,128)S(1)}) custom-call(f32[16,80,128]{2,1,0:T(8,128)} %args_0_.4, f32[16,80,128]{2,1,0:T(8,128)} %args_1_.4, f32[16,80,128]{2,1,0:T(8,128)} %args_2_.4, s32[80,128]{1,0:T(8,128)} %args_3_.4, f32[16]{0:T(128)} %args_4_.4, ...), custom_call_target="tpu_custom_call" | custom-call | tf_op jit(solution)/shard_map/pallas_call | solution.py:822
  26.1 1.3 %shard_map.165 = (f32[16,80,128]{2,1,0:T(8,128)}, f32[16,80,128]{2,1,0:T(8,128)}, f32[16,80,128]{2,1,0:T(8,128)}, f32[40,256]{1,0:T(8,128)}, f32[40,256]{1,0:T(8,128)}) custom-call(f32[16,80,128]{2,1,0:T(8,128)S(1)} %get-tuple-element.9.tracer, f32[16,80,128]{2,1,0:T(8,128)S(1)} %get-tuple-element.10.ocean_u, f32[16,80,128]{2,1,0:T(8,128)S(1)} %get-tuple-element.11.ocean_v, ...), custom_call_target="tpu_custom_call" | custom-call | tf_op jit(solution)/shard_map/pallas_call | solution.py:906

commit v6 on v5

--- a/solution.py
+++ b/solution.py
@@ -64,6 +64,8 @@
     SS,
     S2,
     SS2,
+    FR,
+    FO,
     PE,
     PW,
     EB,
@@ -550,21 +552,21 @@
 
     lax.fori_loop(0, NF, rim_unpack, 0, unroll=7)
 
-    def inside_of(i):
-        return IDX[:, COLS * i : COLS * (i + 1)]
-
-    def fold_block(ref, f, i, sign):
-        j = BLOCKS - 1 - i
-        value = ref[f, :, COLS * j : COLS * (j + 1)]
-        taken = jnp.take_along_axis(value, inside_of(i), axis=1, mode="promise_in_bounds")
-        return taken if sign > 0 else -taken
-
-    def close_top(ref, f, strip_ref, sf, sign):
-        own = fold_block(strip_ref, sf, REACH, sign)
-        to_the_e = fold_block(strip_ref, sf, REACH + 1, sign)
-        to_the_w = fold_block(strip_ref, sf, REACH - 1, sign)
-        ref[f, 24:25, 0:COLS] = own[7:8]
-        ref[f, 24:25, COLS : 2 * COLS] = jnp.where(lane < COLS // 2, to_the_e, to_the_w)[7:8]
+    fold_blocks = (REACH - 1, REACH, REACH + 1, *range(SIDE, BLOCKS))
+
+    def block_row(ref, f, i):
+        return ref[f, 7:8, COLS * i : COLS * (i + 1)]
+
+    def fold(ref, fields, sign):
+        for p, f in enumerate(fields):
+            for j, i in enumerate(fold_blocks):
+                FR[p, j : j + 1, :] = block_row(ref, f, BLOCKS - 1 - i)
+            taken = jnp.take_along_axis(FR[p], IDX[...], axis=1, mode="promise_in_bounds")
+            FO[p] = taken if sign > 0 else -taken
+
+    def close_top(ref, p):
+        ref[p, 24:25, 0:COLS] = FO[p, 1:2, :]
+        ref[p, 24:25, COLS : 2 * COLS] = jnp.where(lane < COLS // 2, FO[p, 2:3, :], FO[p, 0:1, :])
 
     def window(first, reach):
         middle = first + REACH
@@ -572,7 +574,7 @@
         wide_low, wide_high = max(low - 1, first), min(high + 1, first + SIDE)
         return low, high, wide_low, wide_high
 
-    def strip_sides(ref, f, win, sign):
+    def strip_sides(ref, f, win, p):
         low, high, wide_low, wide_high = win
         wide = ref[f, :, COLS * wide_low : COLS * wide_high]
         length = COLS * (wide_high - wide_low)
@@ -580,7 +582,7 @@
         value = wide[:, cut]
         to_east = pltpu.roll(wide, length - 1, 1)[:, cut]
         to_west = pltpu.roll(wide, 1, 1)[:, cut]
-        folded = jnp.concatenate([fold_block(ref, f, i, sign) for i in range(low, high)], axis=1)
+        folded = jnp.concatenate([FO[p, j : j + 1, :] for j in map(fold_blocks.index, range(low, high))], axis=1)
         to_north = jnp.where(row8 == 7, folded, pltpu.roll(value, 7, 0))
         to_south = pltpu.roll(value, 1, 0)
         return value, to_east, to_west, to_north, to_south
@@ -661,19 +663,21 @@
         vel, sig, i_a, i_b = (S, SAB, 0, 1) if cycles[0] == 0 else (S2, S2, 2, 3)
         for cycle in cycles:
             left = 3 if cycle == cycles[0] else 1
-            close_top(XT, 0, vel, 0, -1)
-            close_top(XT, 1, vel, 1, -1)
+            fold(vel, (0, 1), -1)
+            close_top(XT, 0)
+            close_top(XT, 1)
             for win in windows(left):
                 cols = slice(COLS * win[0], COLS * win[1])
-                u, v = strip_sides(vel, 0, win, -1), strip_sides(vel, 1, win, -1)
+                u, v = strip_sides(vel, 0, win, 0), strip_sides(vel, 1, win, 1)
                 old = (sig[i_a, :, cols], sig[i_b, :, cols]) if cycle else None
                 sig[i_a, :, cols], sig[i_b, :, cols] = stress(u, v, S[3, :, cols], old)
             chunk_stress(XT, ABT, 8, cycle == 0)
-            close_top(ABT, 0, sig, i_a, 1)
-            close_top(ABT, 1, sig, i_b, 1)
+            fold(sig, (i_a, i_b), 1)
+            close_top(ABT, 0)
+            close_top(ABT, 1)
             for win in windows(left - 1):
                 cols = slice(COLS * win[0], COLS * win[1])
-                push(S, vel, every, cols, strip_sides(sig, i_a, win, 1), strip_sides(sig, i_b, win, 1))
+                push(S, vel, every, cols, strip_sides(sig, i_a, win, 0), strip_sides(sig, i_b, win, 1))
             chunk_push(XT, ABT, 8)
 
     for start in chunks:
@@ -689,7 +693,8 @@
     @pl.when(is_top)
     def _():
         strips_arrive(False)
-        IDX[...] = jnp.broadcast_to(S[NF, 7:8, 0 : BLOCKS * COLS], IDX.shape).astype(jnp.int32)
+        for j, i in enumerate(fold_blocks):
+            IDX[j : j + 1, :] = block_row(S, NF, i).astype(jnp.int32)
         ready(S, every, slice(0, BLOCKS * COLS))
         top_cycles((0, 1))
         SS2[0:2] = XT[0:2, high_piece, 0:COLS]
@@ -839,6 +844,8 @@
                 vmem((NS, 8, COLS), f32),
                 vmem((4, 8, 2 * BLOCKS * COLS), f32),
                 vmem((4, 8, COLS), f32),
+                vmem((2, 8, COLS), f32),
+                vmem((2, 8, COLS), f32),
                 vmem((HALF, COLS), f32),
                 vmem((HALF, COLS), f32),
                 vmem((HALF, COLS), f32),
@@ -860,7 +867,7 @@
                 vmem((5, ROWS, COLS), f32),
                 vmem((ROWS, COLS), jnp.int32),
                 vmem((ROWS, COLS), jnp.int32),
-                vmem((8, BLOCKS * COLS), jnp.int32),
+                vmem((8, COLS), jnp.int32),
                 pltpu.SMEM((LEV,), f32),
                 pltpu.SMEM((LEV,), f32),
                 pltpu.SMEM((LEV, LEV), f32),

time: 27.5 us -> 27.4 us (level)
  no operation moved by 1% of the time
where the time goes in v6:
time: 27.4 us; the launch traced here: 27.3 us
  Pallas kernels  26.6 us (97%)
  between operations  0.64 us (2%)
    pallas_call x1, Pallas kernels, body(): pl.pallas_call(step, out_shape=(*shapes[:3], jax.ShapeDtypeStruct((2, *ic...  25.3 us
    pallas_call x1, Pallas kernels, body(): pl.pallas_call(deliver, out_shape=shapes, in_specs=[anywhere] * 4, out_sp...  1.32 us

profile of v6, /device:TPU:224, one launch (start us, length us, event | category | flops | bytes accessed | tf_op | source)
XLA Modules:
  0.0 27.3 jit_solution(4714758536717323496)
XLA Ops:
  0.6 25.3 %shard_map.164 = (f32[16,80,128]{2,1,0:T(8,128)S(1)}, f32[16,80,128]{2,1,0:T(8,128)S(1)}, f32[16,80,128]{2,1,0:T(8,128)S(1)}, f32[2,40,256]{2,1,0:T(8,128)S(1)}) custom-call(f32[16,80,128]{2,1,0:T(8,128)} %args_0_.4, f32[16,80,128]{2,1,0:T(8,128)} %args_1_.4, f32[16,80,128]{2,1,0:T(8,128)} %args_2_.4, s32[80,128]{1,0:T(8,128)} %args_3_.4, f32[16]{0:T(128)} %args_4_.4, ...), custom_call_target="tpu_custom_call" | custom-call | tf_op jit(solution)/shard_map/pallas_call | solution.py:827
  25.9 1.3 %shard_map.165 = (f32[16,80,128]{2,1,0:T(8,128)}, f32[16,80,128]{2,1,0:T(8,128)}, f32[16,80,128]{2,1,0:T(8,128)}, f32[40,256]{1,0:T(8,128)}, f32[40,256]{1,0:T(8,128)}) custom-call(f32[16,80,128]{2,1,0:T(8,128)S(1)} %get-tuple-element.9.tracer, f32[16,80,128]{2,1,0:T(8,128)S(1)} %get-tuple-element.10.ocean_u, f32[16,80,128]{2,1,0:T(8,128)S(1)} %get-tuple-element.11.ocean_v, ...), custom_call_target="tpu_custom_call" | custom-call | tf_op jit(solution)/shard_map/pallas_call | solution.py:913

commit v7 on v6

--- a/solution.py
+++ b/solution.py
@@ -290,37 +290,6 @@
     def _():
         first_f.start()
 
-    load_t.wait()
-    for f in range(3 * LEV):
-        TR[f : f + 1, :] = F[f, 87:88, :]
-        BR[f : f + 1, :] = F[f, 8:9, :]
-    row_n = send(TR, SR, edge_send.at[2], edge_recv.at[2], at(me, gy + 1))
-    row_s = send(BR, NR, edge_send.at[3], edge_recv.at[3], at(me, gy - 1))
-    row_f = send(TR, NR, edge_send.at[4], edge_recv.at[4], at(mirror, gy))
-
-    @pl.when(has_north)
-    def _():
-        row_n.start()
-
-    @pl.when(has_south)
-    def _():
-        row_s.start()
-
-    @pl.when(is_top)
-    def _():
-        row_f.start()
-
-    def pack(f, packed):
-        return jnp.where((lane >> 1) == f, pltpu.roll(F[f, 8 : 8 + ROWS, :], 2 * f + 1, 1), packed)
-
-    packed = lax.fori_loop(0, 3 * LEV, pack, jnp.zeros((ROWS, COLS), jnp.float32), unroll=3)
-    CE[...] = jnp.where(even, packed[0:HALF], pltpu.roll(packed[HALF:ROWS], 1, 1))
-    CW[...] = jnp.where(even, pltpu.roll(packed[HALF:ROWS], COLS - 1, 1), packed[0:HALF])
-    col_to_e = send(CE, RW, edge_send.at[0], edge_recv.at[0], at(east, gy))
-    col_to_w = send(CW, RE, edge_send.at[1], edge_recv.at[1], at(west, gy))
-    col_to_e.start()
-    col_to_w.start()
-
     lane2 = lax.broadcasted_iota(jnp.int32, (LEV, LEV * LEV), 1)
     weights = jnp.zeros((LEV, LEV * LEV), jnp.float32)
     for l in range(LEV):
@@ -481,43 +450,36 @@
         S[:, :, middle] = SS[...]
         strips_start(False)
 
-    col_to_e.wait()
-    col_to_w.wait()
+    load_t.wait()
+    for f in range(3 * LEV):
+        TR[f : f + 1, :] = F[f, 87:88, :]
+        BR[f : f + 1, :] = F[f, 8:9, :]
+    row_n = send(TR, SR, edge_send.at[2], edge_recv.at[2], at(me, gy + 1))
+    row_s = send(BR, NR, edge_send.at[3], edge_recv.at[3], at(me, gy - 1))
+    row_f = send(TR, NR, edge_send.at[4], edge_recv.at[4], at(mirror, gy))
 
     @pl.when(has_north)
     def _():
-        row_n.wait_send()
-        row_s.wait_recv()
+        row_n.start()
 
     @pl.when(has_south)
     def _():
-        row_s.wait_send()
-        row_n.wait_recv()
-
-    @pl.when(is_top)
-    def _():
-        row_f.wait()
-        inside = jnp.broadcast_to(inside_here, (8, COLS))
-        for r in range(0, 3 * LEV, 8):
-            taken = jnp.take_along_axis(NR[r : r + 8, :], inside, axis=1, mode="promise_in_bounds")
-            NR[r : r + 8, :] = taken if r < LEV else -taken
-
-    for f in range(3 * LEV):
-        F[f, 88:89, :] = NR[f : f + 1, :]
-        F[f, 7:8, :] = SR[f : f + 1, :]
-    GE[0:HALF] = jnp.where(even, pltpu.roll(RE[...], COLS - 1, 1), pltpu.roll(RW[...], 1, 1))
-    GE[HALF:ROWS] = jnp.where(even, RE[...], RW[...])
-
-    def diffuse(f, carry):
-        coefficient = jnp.where(f < LEV, diffusivity[f & (LEV - 1)], viscosity[f & (LEV - 1)])
-        value, spread = lap(f, pltpu.roll(GE[...], COLS - 1 - 2 * f, 1))
-        new = value + coefficient * spread
-        high = new.astype(jnp.bfloat16)
-        DH[f] = high
-        DL[f] = (new - high.astype(jnp.float32)).astype(jnp.bfloat16)
-        return carry
-
-    lax.fori_loop(0, 2 * LEV, diffuse, 0, unroll=4)
+        row_s.start()
+
+    @pl.when(is_top)
+    def _():
+        row_f.start()
+
+    def pack(f, packed):
+        return jnp.where((lane >> 1) == f, pltpu.roll(F[f, 8 : 8 + ROWS, :], 2 * f + 1, 1), packed)
+
+    packed = lax.fori_loop(0, 3 * LEV, pack, jnp.zeros((ROWS, COLS), jnp.float32), unroll=3)
+    CE[...] = jnp.where(even, packed[0:HALF], pltpu.roll(packed[HALF:ROWS], 1, 1))
+    CW[...] = jnp.where(even, pltpu.roll(packed[HALF:ROWS], COLS - 1, 1), packed[0:HALF])
+    col_to_e = send(CE, RW, edge_send.at[0], edge_recv.at[0], at(east, gy))
+    col_to_w = send(CW, RE, edge_send.at[1], edge_recv.at[1], at(west, gy))
+    col_to_e.start()
+    col_to_w.start()
 
     to_e.wait()
     to_w.wait()
@@ -725,6 +687,44 @@
     def _():
         vel_away[1].start()
         vel_here.start()
+
+    col_to_e.wait()
+    col_to_w.wait()
+
+    @pl.when(has_north)
+    def _():
+        row_n.wait_send()
+        row_s.wait_recv()
+
+    @pl.when(has_south)
+    def _():
+        row_s.wait_send()
+        row_n.wait_recv()
+
+    @pl.when(is_top)
+    def _():
+        row_f.wait()
+        inside = jnp.broadcast_to(inside_here, (8, COLS))
+        for r in range(0, 3 * LEV, 8):
+            taken = jnp.take_along_axis(NR[r : r + 8, :], inside, axis=1, mode="promise_in_bounds")
+            NR[r : r + 8, :] = taken if r < LEV else -taken
+
+    for f in range(3 * LEV):
+        F[f, 88:89, :] = NR[f : f + 1, :]
+        F[f, 7:8, :] = SR[f : f + 1, :]
+    GE[0:HALF] = jnp.where(even, pltpu.roll(RE[...], COLS - 1, 1), pltpu.roll(RW[...], 1, 1))
+    GE[HALF:ROWS] = jnp.where(even, RE[...], RW[...])
+
+    def diffuse(f, carry):
+        coefficient = jnp.where(f < LEV, diffusivity[f & (LEV - 1)], viscosity[f & (LEV - 1)])
+        value, spread = lap(f, pltpu.roll(GE[...], COLS - 1 - 2 * f, 1))
+        new = value + coefficient * spread
+        high = new.astype(jnp.bfloat16)
+        DH[f] = high
+        DL[f] = (new - high.astype(jnp.float32)).astype(jnp.bfloat16)
+        return carry
+
+    lax.fori_loop(0, 2 * LEV, diffuse, 0, unroll=4)
 
     def regrid(g):
         planes = pl.ds(g * LEV, LEV)

time: 27.4 us -> 27.3 us (level)
  no operation moved by 1% of the time
where the time goes in v7:
time: 27.3 us; the launch traced here: 27.2 us
  Pallas kernels  26.6 us (97%)
  between operations  0.64 us (2%)
    pallas_call x1, Pallas kernels, body(): pl.pallas_call(step, out_shape=(*shapes[:3], jax.ShapeDtypeStruct((2, *ic...  25.3 us
    pallas_call x1, Pallas kernels, body(): pl.pallas_call(deliver, out_shape=shapes, in_specs=[anywhere] * 4, out_sp...  1.32 us

profile of v7, /device:TPU:224, one launch (start us, length us, event | category | flops | bytes accessed | tf_op | source)
XLA Modules:
  0.0 27.2 jit_solution(18301216102482001338)
XLA Ops:
  0.6 25.3 %shard_map.164 = (f32[16,80,128]{2,1,0:T(8,128)S(1)}, f32[16,80,128]{2,1,0:T(8,128)S(1)}, f32[16,80,128]{2,1,0:T(8,128)S(1)}, f32[2,40,256]{2,1,0:T(8,128)S(1)}) custom-call(f32[16,80,128]{2,1,0:T(8,128)} %args_0_.4, f32[16,80,128]{2,1,0:T(8,128)} %args_1_.4, f32[16,80,128]{2,1,0:T(8,128)} %args_2_.4, s32[80,128]{1,0:T(8,128)} %args_3_.4, f32[16]{0:T(128)} %args_4_.4, ...), custom_call_target="tpu_custom_call" | custom-call | tf_op jit(solution)/shard_map/pallas_call | solution.py:827
  25.9 1.3 %shard_map.165 = (f32[16,80,128]{2,1,0:T(8,128)}, f32[16,80,128]{2,1,0:T(8,128)}, f32[16,80,128]{2,1,0:T(8,128)}, f32[40,256]{1,0:T(8,128)}, f32[40,256]{1,0:T(8,128)}) custom-call(f32[16,80,128]{2,1,0:T(8,128)S(1)} %get-tuple-element.9.tracer, f32[16,80,128]{2,1,0:T(8,128)S(1)} %get-tuple-element.10.ocean_u, f32[16,80,128]{2,1,0:T(8,128)S(1)} %get-tuple-element.11.ocean_v, ...), custom_call_target="tpu_custom_call" | custom-call | tf_op jit(solution)/shard_map/pallas_call | solution.py:913
